TPU v7x, 32 devices: a whole 2x2x4 slice. The times are simulated.
32 devices in a mesh: node: 8 (over y, x, core), centre: 4 (over z).
Axes of the slice: x: 2, y: 2, z: 4, core: 2. Of those that a mesh axis runs over, the one named last changes fastest.
Arguments:
- node_coords: float32 [3, 32768], P(None, ('node', 'centre')), may hold values from 0 to 1
- centre_coords: float32 [3, 16384], P(None, ('centre', 'node')), may hold values from 0 to 1
- disp_coef: float32 [6, 16384], P(None, ('centre', 'node')), may hold values from -3 to 3
- send_count: int32 [8, 8], P('node'), may hold values from 1 to 1024, 4096 in all within a row
- send_order: int32 [8, 4096], P('node'), may hold values from 0 to 4095, each once within a row
- slot_perm: int32 [8, 8192], P('node'), may hold values from 0 to 8191, each once within a row
- fluid_force: float32 [3, 65536], P(None, 'node'), may hold values from -2 to 2
Outputs:
- fluid_disp: float32 [6, 65536], P(None, 'node')
- centre_force: float32 [3, 16384], P(None, ('centre', 'node'))
Inputs may be any that keep to these rules, and one draw needn't show every extreme that they name: `send_count`: each row sums to 4096; each row's largest entry is 1024. `send_order`: each row is a permutation. `slot_perm`: each row is a permutation.
All inputs are finite; a program needn't handle non-finite values.
Results may differ from a plain program's by a relative error of at most 0.0003.
Values sent between devices are 32-bit elements; how exact they have to be, the bound alone decides.
A program may use at most 64 MiB of HBM per device.

v0:
```python
import math

import jax
import jax.numpy as jnp
from jax import lax
from jax.sharding import PartitionSpec as P

SUPPORT = 192


def kernel(points, centres, radius):
    squared = (points[0][:, None] - centres[0][None, :]) ** 2
    squared = squared + (points[1][:, None] - centres[1][None, :]) ** 2
    squared = squared + (points[2][:, None] - centres[2][None, :]) ** 2
    scaled = jnp.sqrt(squared) / radius
    remain = jnp.maximum(1.0 - scaled, 0.0)
    return remain**4 * (4.0 * scaled + 1.0)


def body(node_coords, centre_coords, disp_coef, send_count, send_order, slot_perm, fluid_force):
    n_node = lax.axis_size("node")
    n_centre = lax.axis_size("centre")
    node_dev = send_order.shape[1]
    fluid_dev = slot_perm.shape[1]
    capacity = fluid_dev // n_node
    centre_total = centre_coords.shape[1] * n_node * n_centre
    radius = (0.75 * SUPPORT / (math.pi * centre_total)) ** (1.0 / 3.0)
    points = lax.all_gather(node_coords, "centre", axis=1, tiled=True)
    centres, coeffs = (
        lax.all_gather(centre_coords, "node", axis=1, tiled=True),
        lax.all_gather(disp_coef, "node", axis=1, tiled=True),
    )
    counts = send_count[0]
    offsets = jnp.cumsum(counts) - counts
    slot_ids = jnp.arange(capacity, dtype=jnp.int32)
    filled = (slot_ids[None, :] < counts[:, None]).reshape(-1)
    places = jnp.minimum(offsets[:, None] + slot_ids[None, :], node_dev - 1).reshape(-1)
    picked = send_order[0][places]
    ordering = slot_perm[0]
    block_rows = math.gcd(node_dev, 512)
    point_blocks = jnp.transpose(points.reshape(3, node_dev // block_rows, block_rows), (1, 0, 2))
    zero_sum = jnp.zeros((3, centres.shape[1]), jnp.float32)

    def displace(basis):
        return lax.dot_general(
            coeffs,
            basis,
            (((1,), (1,)), ((), ())),
            precision=lax.Precision.HIGHEST,
            preferred_element_type=jnp.float32,
        )

    def accumulate(running, forces, basis):
        return running + jnp.dot(
            forces, basis, precision=lax.Precision.HIGHEST, preferred_element_type=jnp.float32
        )

    def disp_pass(block_pts):
        return displace(kernel(block_pts, centres, radius))

    disp_blocks = lax.map(disp_pass, point_blocks)
    inverse = jnp.argsort(ordering)
    incoming = lax.all_to_all(
        fluid_force[:, inverse], "node", split_axis=1, concat_axis=1, tiled=True
    )
    masked = jnp.where(filled[None, :], incoming, 0.0)
    wall_force = jnp.zeros((3, node_dev), jnp.float32).at[:, picked].add(masked)
    force_blocks = jnp.transpose(
        wall_force.reshape(3, node_dev // block_rows, block_rows), (1, 0, 2)
    )

    def force_pass(running, pieces):
        return (accumulate(running, pieces[1], kernel(pieces[0], centres, radius)), None)

    force_total, unused = lax.scan(force_pass, zero_sum, (point_blocks, force_blocks))
    partial_value = jnp.transpose(disp_blocks, (1, 0, 2)).reshape(6, node_dev)
    summed = lax.psum(partial_value, "centre")
    outgoing = jnp.where(filled[None, :], summed[:, picked], 0.0)
    received = lax.all_to_all(outgoing, "node", split_axis=1, concat_axis=1, tiled=True)
    fluid_disp = received[:, ordering]
    centre_force = lax.psum_scatter(force_total, "node", scatter_dimension=1, tiled=True)
    return (fluid_disp, centre_force)


def solution(mesh):
    placed = (
        P(None, ("node", "centre")),
        P(None, ("centre", "node")),
        P(None, ("centre", "node")),
        P("node", None),
        P("node", None),
        P("node", None),
        P(None, "node"),
    )
    return jax.shard_map(
        body,
        mesh=mesh,
        in_specs=placed,
        out_specs=(P(None, "node"), P(None, ("centre", "node"))),
        check_vma=False,
    )
```

profile of v0, /device:TPU:0, one launch (start us, length us, event | category | flops | bytes accessed | tf_op | source)
XLA Modules:
  0.0 465.7 jit_solution(3908440139953812652)
XLA Ops:
  8.0 0.0 copy-start
  8.0 0.0 copy-start.1
  8.0 0.0 copy-start.4
  8.0 0.0 copy-start.2
  8.0 0.0 copy-start.3
  8.1 3.5 copy.27
  11.5 0.0 copy-done.1
  11.5 6.8 %sort.17 = (s32[8192]{0:T(1024)}, s32[8192]{0:T(1024)S(1)}) sort(s32[8192]{0:T(1024)S(1)} %bitcast.113, s32[8192]{0:T(1024)S(1)} %iota.9), dimensions={0}, to_apply=%region_4.5 | sort | flops 106496 | bytes 131072 | tf_op jit(solution)/shard_map/jit(argsort)/sort | solution.py:62
  18.3 29.9 %gather_fusion.3 = f32[8192,3]{1,0:T(8,128)} fusion(f32[3,8192]{0,1:T(8,128)} %copy.27, s32[8192]{0:T(1024)S(1)} %fusion.78), kind=kCustom, calls=%fused_computation.3 | custom fusion | bytes 229376 | tf_op jit(solution)/shard_map/gather | solution.py:64
  48.2 3.5 copy.28
  51.7 5.2 %all-to-all-start.1 = ((f32[3,8,1024]{2,0,1:T(4,128)}), f32[3,8,1024]{2,0,1:T(4,128)S(1)}, u32[]{:S(2)}, u32[]{:S(2)}) async-start(f32[3,8,1024]{2,0,1:T(4,128)} %copy.28), calls=%async_computation.1 | async-start | bytes 262144 | tf_op jit(solution)/shard_map/all_to_all | solution.py:63
  56.8 0.0 all-reduce.2.cloned.1.call-start
  56.9 0.0 copy-done.4
  56.9 9.7 %all_gather.10 = f32[3,4096]{1,0:T(4,128)S(1)} all-gather(f32[3,512]{1,0:T(4,128)S(1)} %copy-done.4), channel_id=1, replica_groups=mesh['node'=8,'centre'=4] {'node'}, dimensions={1}, use_global_device_ids=true | all-gather | bytes 55296 | tf_op jit(solution)/shard_map/all_gather | solution.py:30
  66.6 0.0 copy-done.2
  66.6 13.3 %all_gather.9 = f32[3,4096]{1,0:T(4,128)S(1)} all-gather(f32[3,1024]{1,0:T(4,128)S(1)} %copy-done.2), channel_id=1, replica_groups=mesh['node'=8,'centre'=4] {'centre'}, dimensions={1}, use_global_device_ids=true | all-gather | bytes 61440 | tf_op jit(solution)/shard_map/all_gather | solution.py:28
  79.9 0.0 copy-done.3
  79.9 9.2 %all_gather.11 = f32[6,4096]{1,0:T(8,128)S(1)} all-gather(f32[6,512]{1,0:T(8,128)S(1)} %copy-done.3), channel_id=1, replica_groups=mesh['node'=8,'centre'=4] {'node'}, dimensions={1}, use_global_device_ids=true | all-gather | bytes 110592 | tf_op jit(solution)/shard_map/all_gather | solution.py:31
  89.1 106.7 %while.25 = (s32[]{:T(128)}, f32[8,6,512]{2,1,0:T(8,128)S(1)}, f32[8,3,512]{2,1,0:T(4,128)S(1)}, f32[3,4096]{1,0:T(4,128)S(1)}, f32[6,4096]{1,0:T(8,128)S(1)}, /*index=5*/s32[]{:T(128)}, s32[]{:T(128)}, s32[]{}, s32[]{}) while((s32[]{:T(128)}, f32[8,6,512]{2,1,0:T(8,128)S(1)}, f32[8,3,512]{2,1,0:T(4,128)S(1)}, f32[3,4096]{1,0:T(4,128)S(1)}, ...), condition=%wide.region_1.2_spmd, body=%wide.region_0.0_spmd.sunk | while | flops 184549376 | bytes 313477 | solution.py:61
  89.1 13.3 %fusion.94 = f32[8,6,512]{2,1,0:T(8,128)S(1)} fusion(f32[8,6,512]{2,1,0:T(8,128)S(1)} %get-tuple-element.292, s32[]{:T(128)} %get-tuple-element.291, f32[6,4096]{1,0:T(8,128)S(1)} %get-tuple-element.304, f32[4096]{0:T(1024)S(1)} %bitcast.108, f32[512]{0:T(512)S(1)} %bitcast.126, f32[4096]{0:T(1024)S(1)} %bitcast.109, f32[512]{0:T(512)S(1)} %bitcast.125, ...), kind=kOutput, calls=%fused_computation.34.clone.1 | convolution fusion | flops 184549376 | bytes 202756 | tf_op jit(solution)/shard_map/while/body/eval_jaxpr/dot_general | solution.py:45
  102.5 13.3 %fusion.94 = f32[8,6,512]{2,1,0:T(8,128)S(1)} fusion(f32[8,6,512]{2,1,0:T(8,128)S(1)} %get-tuple-element.292, s32[]{:T(128)} %get-tuple-element.291, f32[6,4096]{1,0:T(8,128)S(1)} %get-tuple-element.304, f32[4096]{0:T(1024)S(1)} %bitcast.108, f32[512]{0:T(512)S(1)} %bitcast.126, f32[4096]{0:T(1024)S(1)} %bitcast.109, f32[512]{0:T(512)S(1)} %bitcast.125, ...), kind=kOutput, calls=%fused_computation.34.clone.1 | convolution fusion | flops 184549376 | bytes 202756 | tf_op jit(solution)/shard_map/while/body/eval_jaxpr/dot_general | solution.py:45
  115.8 13.3 %fusion.94 = f32[8,6,512]{2,1,0:T(8,128)S(1)} fusion(f32[8,6,512]{2,1,0:T(8,128)S(1)} %get-tuple-element.292, s32[]{:T(128)} %get-tuple-element.291, f32[6,4096]{1,0:T(8,128)S(1)} %get-tuple-element.304, f32[4096]{0:T(1024)S(1)} %bitcast.108, f32[512]{0:T(512)S(1)} %bitcast.126, f32[4096]{0:T(1024)S(1)} %bitcast.109, f32[512]{0:T(512)S(1)} %bitcast.125, ...), kind=kOutput, calls=%fused_computation.34.clone.1 | convolution fusion | flops 184549376 | bytes 202756 | tf_op jit(solution)/shard_map/while/body/eval_jaxpr/dot_general | solution.py:45
  129.2 13.3 %fusion.94 = f32[8,6,512]{2,1,0:T(8,128)S(1)} fusion(f32[8,6,512]{2,1,0:T(8,128)S(1)} %get-tuple-element.292, s32[]{:T(128)} %get-tuple-element.291, f32[6,4096]{1,0:T(8,128)S(1)} %get-tuple-element.304, f32[4096]{0:T(1024)S(1)} %bitcast.108, f32[512]{0:T(512)S(1)} %bitcast.126, f32[4096]{0:T(1024)S(1)} %bitcast.109, f32[512]{0:T(512)S(1)} %bitcast.125, ...), kind=kOutput, calls=%fused_computation.34.clone.1 | convolution fusion | flops 184549376 | bytes 202756 | tf_op jit(solution)/shard_map/while/body/eval_jaxpr/dot_general | solution.py:45
  142.5 13.3 %fusion.94 = f32[8,6,512]{2,1,0:T(8,128)S(1)} fusion(f32[8,6,512]{2,1,0:T(8,128)S(1)} %get-tuple-element.292, s32[]{:T(128)} %get-tuple-element.291, f32[6,4096]{1,0:T(8,128)S(1)} %get-tuple-element.304, f32[4096]{0:T(1024)S(1)} %bitcast.108, f32[512]{0:T(512)S(1)} %bitcast.126, f32[4096]{0:T(1024)S(1)} %bitcast.109, f32[512]{0:T(512)S(1)} %bitcast.125, ...), kind=kOutput, calls=%fused_computation.34.clone.1 | convolution fusion | flops 184549376 | bytes 202756 | tf_op jit(solution)/shard_map/while/body/eval_jaxpr/dot_general | solution.py:45
  155.8 13.3 %fusion.94 = f32[8,6,512]{2,1,0:T(8,128)S(1)} fusion(f32[8,6,512]{2,1,0:T(8,128)S(1)} %get-tuple-element.292, s32[]{:T(128)} %get-tuple-element.291, f32[6,4096]{1,0:T(8,128)S(1)} %get-tuple-element.304, f32[4096]{0:T(1024)S(1)} %bitcast.108, f32[512]{0:T(512)S(1)} %bitcast.126, f32[4096]{0:T(1024)S(1)} %bitcast.109, f32[512]{0:T(512)S(1)} %bitcast.125, ...), kind=kOutput, calls=%fused_computation.34.clone.1 | convolution fusion | flops 184549376 | bytes 202756 | tf_op jit(solution)/shard_map/while/body/eval_jaxpr/dot_general | solution.py:45
  169.2 13.3 %fusion.94 = f32[8,6,512]{2,1,0:T(8,128)S(1)} fusion(f32[8,6,512]{2,1,0:T(8,128)S(1)} %get-tuple-element.292, s32[]{:T(128)} %get-tuple-element.291, f32[6,4096]{1,0:T(8,128)S(1)} %get-tuple-element.304, f32[4096]{0:T(1024)S(1)} %bitcast.108, f32[512]{0:T(512)S(1)} %bitcast.126, f32[4096]{0:T(1024)S(1)} %bitcast.109, f32[512]{0:T(512)S(1)} %bitcast.125, ...), kind=kOutput, calls=%fused_computation.34.clone.1 | convolution fusion | flops 184549376 | bytes 202756 | tf_op jit(solution)/shard_map/while/body/eval_jaxpr/dot_general | solution.py:45
  182.5 13.3 %fusion.94 = f32[8,6,512]{2,1,0:T(8,128)S(1)} fusion(f32[8,6,512]{2,1,0:T(8,128)S(1)} %get-tuple-element.292, s32[]{:T(128)} %get-tuple-element.291, f32[6,4096]{1,0:T(8,128)S(1)} %get-tuple-element.304, f32[4096]{0:T(1024)S(1)} %bitcast.108, f32[512]{0:T(512)S(1)} %bitcast.126, f32[4096]{0:T(1024)S(1)} %bitcast.109, f32[512]{0:T(512)S(1)} %bitcast.125, ...), kind=kOutput, calls=%fused_computation.34.clone.1 | convolution fusion | flops 184549376 | bytes 202756 | tf_op jit(solution)/shard_map/while/body/eval_jaxpr/dot_general | solution.py:45
  195.8 0.0 copy-start.5
  195.8 2.0 copy.24
  197.8 0.0 all-reduce.2.cloned.1.call-update
  197.8 0.0 reduce-scatter.4.cloned.1.call-start
  197.9 0.0 copy-done.5
  197.9 0.2 reduce-window.8
  198.1 0.1 minimum_bitcast_fusion
  198.3 0.0 copy-done
  198.3 45.5 %gather_fusion = s32[8192]{0:T(1024)S(1)} fusion(s32[4096]{0:T(1024)S(1)} %bitcast.95, s32[8192]{0:T(1024)S(1)} %broadcast_clamp_fusion.1), kind=kCustom, calls=%fused_computation | custom fusion | bytes 98304 | tf_op jit(solution)/shard_map/gather | solution.py:38
  243.9 0.1 fusion.79
  244.0 0.0 all-to-all-done.1
  244.1 2.7 copy.29
  246.7 47.1 %scatter_custom_fusion = f32[3,4096]{0,1:T(8,128)S(1)} fusion(s32[8192]{0:T(1024)S(1)} %bitcast.116, f32[8192,3]{1,0:T(8,128)} %copy.29, f32[]{:T(128)} %constant.90.clone.1), kind=kCustom, calls=%fused_computation.81 | custom fusion | flops 24576 | bytes 49664 | tf_op jit(solution)/shard_map/scatter-add | solution.py:67
  293.8 0.6 copy.30
  294.5 82.2 %while.26 = (s32[]{:T(128)}, f32[3,4096]{1,0:T(4,128)S(1)}, f32[8,3,512]{2,1,0:T(4,128)S(1)}, f32[8,3,512]{2,1,0:T(4,128)S(1)}, f32[3,4096]{1,0:T(4,128)S(1)}, /*index=5*/s32[]{:T(128)}, s32[]{:T(128)}, s32[]{}, s32[]{}) while((s32[]{:T(128)}, f32[3,4096]{1,0:T(4,128)S(1)}, f32[8,3,512]{2,1,0:T(4,128)S(1)}, ...), condition=%wide.region_7.8_spmd.clone, body=%wide.region_6.7_spmd.clone.sunk | while | flops 109076480 | bytes 288911 | solution.py:75
  294.7 10.2 %fusion.98 = f32[3,4096]{1,0:T(4,128)S(1)} fusion(f32[4096]{0:T(1024)S(1)} %bitcast.105, f32[512]{0:T(512)S(1)} %bitcast.123, f32[4096]{0:T(1024)S(1)} %bitcast.106, f32[512]{0:T(512)S(1)} %bitcast.122, f32[4096]{0:T(1024)S(1)} %bitcast.104, f32[512]{0:T(512)S(1)} %bitcast.121, f32[3,4096]{1,0:T(4,128)S(1)} %get-tuple-element.319, pred[]{:T(512)S(6)} %compare.7, ...), kind=kOutput, calls=%fused_computation.60.clone.1 | convolution fusion | flops 109076480 | bytes 178181 | tf_op jit(solution)/shard_map/while/body/eval_jaxpr/dot_general | solution.py:54
  305.0 10.2 %fusion.98 = f32[3,4096]{1,0:T(4,128)S(1)} fusion(f32[4096]{0:T(1024)S(1)} %bitcast.105, f32[512]{0:T(512)S(1)} %bitcast.123, f32[4096]{0:T(1024)S(1)} %bitcast.106, f32[512]{0:T(512)S(1)} %bitcast.122, f32[4096]{0:T(1024)S(1)} %bitcast.104, f32[512]{0:T(512)S(1)} %bitcast.121, f32[3,4096]{1,0:T(4,128)S(1)} %get-tuple-element.319, pred[]{:T(512)S(6)} %compare.7, ...), kind=kOutput, calls=%fused_computation.60.clone.1 | convolution fusion | flops 109076480 | bytes 178181 | tf_op jit(solution)/shard_map/while/body/eval_jaxpr/dot_general | solution.py:54
  315.2 10.2 %fusion.98 = f32[3,4096]{1,0:T(4,128)S(1)} fusion(f32[4096]{0:T(1024)S(1)} %bitcast.105, f32[512]{0:T(512)S(1)} %bitcast.123, f32[4096]{0:T(1024)S(1)} %bitcast.106, f32[512]{0:T(512)S(1)} %bitcast.122, f32[4096]{0:T(1024)S(1)} %bitcast.104, f32[512]{0:T(512)S(1)} %bitcast.121, f32[3,4096]{1,0:T(4,128)S(1)} %get-tuple-element.319, pred[]{:T(512)S(6)} %compare.7, ...), kind=kOutput, calls=%fused_computation.60.clone.1 | convolution fusion | flops 109076480 | bytes 178181 | tf_op jit(solution)/shard_map/while/body/eval_jaxpr/dot_general | solution.py:54
  325.5 10.2 %fusion.98 = f32[3,4096]{1,0:T(4,128)S(1)} fusion(f32[4096]{0:T(1024)S(1)} %bitcast.105, f32[512]{0:T(512)S(1)} %bitcast.123, f32[4096]{0:T(1024)S(1)} %bitcast.106, f32[512]{0:T(512)S(1)} %bitcast.122, f32[4096]{0:T(1024)S(1)} %bitcast.104, f32[512]{0:T(512)S(1)} %bitcast.121, f32[3,4096]{1,0:T(4,128)S(1)} %get-tuple-element.319, pred[]{:T(512)S(6)} %compare.7, ...), kind=kOutput, calls=%fused_computation.60.clone.1 | convolution fusion | flops 109076480 | bytes 178181 | tf_op jit(solution)/shard_map/while/body/eval_jaxpr/dot_general | solution.py:54
  335.8 10.2 %fusion.98 = f32[3,4096]{1,0:T(4,128)S(1)} fusion(f32[4096]{0:T(1024)S(1)} %bitcast.105, f32[512]{0:T(512)S(1)} %bitcast.123, f32[4096]{0:T(1024)S(1)} %bitcast.106, f32[512]{0:T(512)S(1)} %bitcast.122, f32[4096]{0:T(1024)S(1)} %bitcast.104, f32[512]{0:T(512)S(1)} %bitcast.121, f32[3,4096]{1,0:T(4,128)S(1)} %get-tuple-element.319, pred[]{:T(512)S(6)} %compare.7, ...), kind=kOutput, calls=%fused_computation.60.clone.1 | convolution fusion | flops 109076480 | bytes 178181 | tf_op jit(solution)/shard_map/while/body/eval_jaxpr/dot_general | solution.py:54
  346.0 10.2 %fusion.98 = f32[3,4096]{1,0:T(4,128)S(1)} fusion(f32[4096]{0:T(1024)S(1)} %bitcast.105, f32[512]{0:T(512)S(1)} %bitcast.123, f32[4096]{0:T(1024)S(1)} %bitcast.106, f32[512]{0:T(512)S(1)} %bitcast.122, f32[4096]{0:T(1024)S(1)} %bitcast.104, f32[512]{0:T(512)S(1)} %bitcast.121, f32[3,4096]{1,0:T(4,128)S(1)} %get-tuple-element.319, pred[]{:T(512)S(6)} %compare.7, ...), kind=kOutput, calls=%fused_computation.60.clone.1 | convolution fusion | flops 109076480 | bytes 178181 | tf_op jit(solution)/shard_map/while/body/eval_jaxpr/dot_general | solution.py:54
  356.3 10.2 %fusion.98 = f32[3,4096]{1,0:T(4,128)S(1)} fusion(f32[4096]{0:T(1024)S(1)} %bitcast.105, f32[512]{0:T(512)S(1)} %bitcast.123, f32[4096]{0:T(1024)S(1)} %bitcast.106, f32[512]{0:T(512)S(1)} %bitcast.122, f32[4096]{0:T(1024)S(1)} %bitcast.104, f32[512]{0:T(512)S(1)} %bitcast.121, f32[3,4096]{1,0:T(4,128)S(1)} %get-tuple-element.319, pred[]{:T(512)S(6)} %compare.7, ...), kind=kOutput, calls=%fused_computation.60.clone.1 | convolution fusion | flops 109076480 | bytes 178181 | tf_op jit(solution)/shard_map/while/body/eval_jaxpr/dot_general | solution.py:54
  366.5 10.2 %fusion.98 = f32[3,4096]{1,0:T(4,128)S(1)} fusion(f32[4096]{0:T(1024)S(1)} %bitcast.105, f32[512]{0:T(512)S(1)} %bitcast.123, f32[4096]{0:T(1024)S(1)} %bitcast.106, f32[512]{0:T(512)S(1)} %bitcast.122, f32[4096]{0:T(1024)S(1)} %bitcast.104, f32[512]{0:T(512)S(1)} %bitcast.121, f32[3,4096]{1,0:T(4,128)S(1)} %get-tuple-element.319, pred[]{:T(512)S(6)} %compare.7, ...), kind=kOutput, calls=%fused_computation.60.clone.1 | convolution fusion | flops 109076480 | bytes 178181 | tf_op jit(solution)/shard_map/while/body/eval_jaxpr/dot_general | solution.py:54
  376.7 2.0 copy.32
  378.7 0.0 reduce-scatter.4.cloned.1.call-update
  378.7 0.0 all-reduce.2.cloned.1.call-done
  378.8 29.3 %gather_fusion.1 = f32[8192,6]{1,0:T(8,128)} fusion(f32[6,4096]{0,1:T(8,128)} %all-reduce.2.cloned.1.call-done, s32[8192]{0:T(1024)S(1)} %broadcast_clamp_fusion.2), kind=kCustom, calls=%fused_computation.1 | custom fusion | bytes 425984 | tf_op jit(solution)/shard_map/gather | solution.py:78
  408.1 2.9 copy.25
  411.0 0.8 broadcast_select_fusion
  411.7 3.4 all-to-all-start
  415.2 4.8 %reduce-scatter.4.cloned.1.call-done = f32[512,3]{1,0:T(8,128)} async-done(((f32[4096,3]{1,0:T(8,128)}), f32[512,3]{1,0:T(8,128)}) %reduce-scatter.4.cloned.1.call-update) | async-done | bytes 6160
  419.9 1.7 copy.33
  421.6 0.7 all-to-all-done
  422.3 2.6 copy.26
  424.9 29.9 %gather_fusion.2 = f32[8192,6]{1,0:T(8,128)} fusion(f32[6,8192]{0,1:T(8,128)} %bitcast.96, s32[8192]{0:T(1024)S(1)} %broadcast_clamp_fusion), kind=kCustom, calls=%fused_computation.2 | custom fusion | bytes 425984 | tf_op jit(solution)/shard_map/gather | solution.py:80
  454.8 3.5 copy.31
  (46 shorter events, 1.1 us)
Async XLA Ops:
  8.0 190.3 %copy-start = (s32[1,4096]{1,0:T(1,128)S(1)}, s32[1,4096]{1,0:T(1,128)}, u32[]{:S(2)}) copy-start(s32[1,4096]{1,0:T(1,128)} %param.15) | copy-start | bytes 49156
  8.0 3.5 copy-start.1
  8.0 48.9 %copy-start.4 = (f32[3,512]{1,0:T(4,128)S(1)}, f32[3,512]{1,0:T(4,128)}, u32[]{:S(2)}) copy-start(f32[3,512]{1,0:T(4,128)} %param.12) | copy-start | bytes 18436
  8.0 58.6 %copy-start.2 = (f32[3,1024]{1,0:T(4,128)S(1)}, f32[3,1024]{1,0:T(4,128)}, u32[]{:S(2)}) copy-start(f32[3,1024]{1,0:T(4,128)} %param.11) | copy-start | bytes 36868
  8.0 71.9 %copy-start.3 = (f32[6,512]{1,0:T(8,128)S(1)}, f32[6,512]{1,0:T(8,128)}, u32[]{:S(2)}) copy-start(f32[6,512]{1,0:T(8,128)} %param.13) | copy-start | bytes 36868
  51.7 192.3 %all-to-all-start.1 = ((f32[3,8,1024]{2,0,1:T(4,128)}), f32[3,8,1024]{2,0,1:T(4,128)S(1)}, u32[]{:S(2)}, u32[]{:S(2)}) async-start(f32[3,8,1024]{2,0,1:T(4,128)} %copy.28), calls=%async_computation.1 | async-start | bytes 262144 | tf_op jit(solution)/shard_map/all_to_all | solution.py:63
  56.8 321.9 %all-reduce.2.cloned.1.call-start = ((), (), s32[]{:S(2)}) async-start(), calls=%async_computation.3 | async-start | bytes 4194304 | tf_op jit(solution)/shard_map/psum | solution.py:77
  195.8 2.1 copy-start.5
  197.8 222.1 %reduce-scatter.4.cloned.1.call-start = ((), (), s32[]{:S(2)}) async-start(), calls=%async_computation.4 | async-start | bytes 2359296
  411.7 10.6 %all-to-all-start = ((f32[6,8,1024]{2,0,1:T(8,128)}), f32[6,8,1024]{2,0,1:T(8,128)S(1)}, u32[]{:S(2)}, u32[]{:S(2)}) async-start(f32[6,8,1024]{2,0,1:T(8,128)} %broadcast_select_fusion), calls=%async_computation | async-start | bytes 524288 | tf_op jit(solution)/shard_map/all_to_all | solution.py:79
Sparse Core Ops, SparseCore 0:
  197.9 86.7 all-reduce.1
Sparse Core Ops, SparseCore 1:
  378.8 41.1 reduce-scatter.3
where the time goes:
time: 466 us
  matrix products  188 us (40%)
  local copies, waits for them, and re-layouts  160 us (34%)
  other arithmetic  55.1 us (12%)
  blocking collectives  32.2 us (7%)
  between operations  15.7 us (3%)
  starting transfers between devices  8.66 us (2%)
  waiting for transfers between devices  5.54 us (1%)
    dot_general x8, matrix products, displace(): lax.dot_general(coeffs, basis, (((1,), (1,)), ((), ())), precision=lax.Pr...  106 us
    dot_general x8, matrix products, accumulate(): jnp.dot(forces, basis, precision=lax.Precision.HIGHEST, preferred_element...  81.5 us
    scatter-add x1, other arithmetic, body(): wall_force = jnp.zeros((3, node_dev), jnp.float32).at[:, picked].add(masked)  47.1 us
    gather x1, local copies, waits for them, and re-layouts, body(): picked = send_order[0][places]  45.5 us
    gather x2, local copies, waits for them, and re-layouts, body(): outgoing = jnp.where(filled[None, :], summed[:, picked], 0.0)  32.2 us
    gather x1, local copies, waits for them, and re-layouts, body(): fluid_force[:, inverse]  29.9 us
    gather x1, local copies, waits for them, and re-layouts, body(): fluid_disp = received[:, ordering]  29.9 us
    all_gather x1, blocking collectives, body(): points = lax.all_gather(node_coords, 'centre', axis=1, tiled=True)  13.3 us
  transfers between devices with their start and end apart: 4, of which 2 were waited for; matrix products, arithmetic and copies ran while one was open for 69% of the time, Pallas kernels for 0%

commit v1 on v0

v1 whole, which is shorter than its diff:
```python
import functools
import math

import jax
import jax.numpy as jnp
from jax import lax
from jax.experimental import pallas as pl
from jax.experimental.pallas import tpu as pltpu
from jax.sharding import PartitionSpec as P

SUPPORT = 192
LANES = 128
F32 = jnp.float32
BF16 = jnp.bfloat16
VMEM_BYTES = 48 * 1024 * 1024
NT = (((1,), (1,)), ((), ()))


def vmem():
    return pl.BlockSpec(memory_space=pltpu.VMEM)


def smem():
    return pl.BlockSpec(memory_space=pltpu.SMEM)


def split(value):
    high = value.astype(BF16).astype(F32)
    return high, value - high


def onehot(index, rows):
    lanes = index.shape[1]
    return jnp.where(lax.broadcasted_iota(jnp.int32, (rows, lanes), 0) == index, 1.0, 0.0)


def scatter_part(values, index, high_rows):
    n = index.shape[1]
    low = jnp.bitwise_and(index, LANES - 1)
    high = lax.shift_right_arithmetic(index, 7)
    low_hot = onehot(low, LANES).astype(BF16)
    mask = lax.broadcasted_iota(jnp.int32, (high_rows, n), 0) == high
    stacked = jnp.concatenate(
        [jnp.where(mask, value, 0.0).astype(BF16) for value in values], axis=0
    )
    return lax.dot_general(stacked, low_hot, NT, preferred_element_type=F32)


def gather_part(lhs, index, high_rows, channels):
    n = index.shape[1]
    low = jnp.bitwise_and(index, LANES - 1)
    high = lax.shift_right_arithmetic(index, 7)
    hot = onehot(high, high_rows).astype(BF16)
    hot = jnp.concatenate([hot, hot], axis=0)
    wide = jnp.dot(lhs, hot, preferred_element_type=F32)
    mask = lax.broadcasted_iota(jnp.int32, (LANES, n), 0) == low
    rows = [
        jnp.sum(
            jnp.where(mask, wide[c * LANES : (c + 1) * LANES], 0.0), axis=0, keepdims=True
        )
        for c in range(channels)
    ]
    return jnp.concatenate(rows, axis=0)


def prepare_kernel(n_node, rows, count_ref, order_ref, perm_ref, force_ref, send_ref, index_ref, acc_ref):
    fluid_dev = perm_ref.shape[1]
    high_rows = fluid_dev // LANES
    node_rows = order_ref.shape[0]
    capacity = rows * LANES
    step = 1024
    for start in range(0, fluid_dev, step):
        values = []
        for c in range(3):
            values.extend(split(force_ref[c : c + 1, start : start + step]))
        part = scatter_part(values, perm_ref[:, start : start + step], high_rows)
        if start == 0:
            acc_ref[...] = part
        else:
            acc_ref[...] += part
    for c in range(3):
        base = 2 * c * high_rows
        for b in range(n_node):
            lo = base + b * rows
            send_ref[b, c * rows : (c + 1) * rows, :] = (
                acc_ref[lo : lo + rows, :]
                + acc_ref[lo + high_rows : lo + high_rows + rows, :]
            )
    high, low = split(order_ref[...].astype(F32))
    lhs = jnp.transpose(
        jnp.concatenate([high, low, jnp.zeros((LANES - 2 * node_rows, LANES), F32)], axis=0)
    ).astype(BF16)[:, : 2 * node_rows]
    offset = jnp.int32(0)
    for o in range(n_node):
        count = count_ref[0, o]
        slot = lax.broadcasted_iota(jnp.int32, (1, capacity), 1)
        place = jnp.minimum(offset + slot, node_rows * LANES - 1)
        found = gather_part(lhs, place, node_rows, 1).astype(jnp.int32)
        found = jnp.where(slot < count, found, -1)
        index_ref[:, o * capacity : (o + 1) * capacity] = found
        offset = offset + count


def greet(axes):
    barrier = pltpu.get_barrier_semaphore()
    total = 0
    for name, size in axes:
        me = lax.axis_index(name)
        for d in range(1, size):
            pl.semaphore_signal(
                barrier, inc=1, device_id={name: lax.rem(me + d, size)},
                device_id_type=pl.DeviceIdType.MESH,
            )
            total += 1
    pl.semaphore_wait(barrier, total)


def spread(name, size, source, target, send_sem, recv_sem, gather):
    me = lax.axis_index(name)
    copies = []
    for d in range(1, size):
        peer = lax.rem(me + d, size)
        copy = pltpu.make_async_remote_copy(
            src_ref=source if gather else source.at[peer],
            dst_ref=target.at[me],
            send_sem=send_sem.at[d],
            recv_sem=recv_sem.at[d],
            device_id={name: peer},
            device_id_type=pl.DeviceIdType.MESH,
        )
        copy.start()
        copies.append(copy)
    return copies


def gather_kernel(
    n_node, n_centre, node_ref, centre_ref, coef_ref, send_ref,
    points_ref, centres_ref, coeffs_ref, recv_ref, sem_a, sem_b, sem_c, sem_d,
):
    greet((("node", n_node), ("centre", n_centre)))
    copies = spread("centre", n_centre, node_ref, points_ref, sem_a.at[0], sem_a.at[1], True)
    copies += spread("node", n_node, centre_ref, centres_ref, sem_b.at[0], sem_b.at[1], True)
    copies += spread("node", n_node, coef_ref, coeffs_ref, sem_c.at[0], sem_c.at[1], True)
    copies += spread("node", n_node, send_ref, recv_ref, sem_d.at[0], sem_d.at[1], False)
    me_node, me_centre = lax.axis_index("node"), lax.axis_index("centre")
    points_ref[me_centre] = node_ref[...]
    centres_ref[me_node] = centre_ref[...]
    coeffs_ref[me_node] = coef_ref[...]
    recv_ref[me_node] = send_ref[me_node]
    for copy in copies:
        copy.wait()


def factor_rows(ref, coords, lanes, left):
    high, rest = split(coords)
    middle, low = split(rest)
    square = jnp.sum(coords * coords, axis=0, keepdims=True)
    scale = 1.0 if left else -2.0
    high, middle, low = high * scale, middle * scale, low * scale
    order = (high, high, middle, middle, high, low) if left else (high, middle, high, middle, low, high)
    for i, piece in enumerate(order):
        ref[3 * i : 3 * i + 3, lanes] = piece
    s_high, s_rest = split(square)
    s_middle, s_low = split(s_rest)
    base = 18 if left else 21
    for i, piece in enumerate((s_high, s_middle, s_low)):
        ref[base + i : base + i + 1, lanes] = piece
    base = 21 if left else 18
    ref[base : base + 3, lanes] = jnp.ones((3, square.shape[1]), F32)


def pair_kernel(
    n_node, n_centre, rows, radius, points_ref, centres_ref, coeffs_ref, recv_ref, index_ref,
    disp_ref, total_ref,
    wide_ref, left_ref, right_ref, coef_ref, force_ref, acc_ref, facc_ref, dacc_ref,
):
    node_part = points_ref.shape[2]
    node_dev = node_part * n_centre
    centre_part = centres_ref.shape[2]
    centre_dev = centre_part * n_node
    node_rows = node_dev // LANES
    capacity = rows * LANES
    inverse = 1.0 / radius
    for o in range(n_node):
        values = []
        for c in range(3):
            row = jnp.concatenate(
                [recv_ref[o, c * rows + r : c * rows + r + 1, :] for r in range(rows)], axis=1
            )
            values.append(split(row))
        values = [v[0] for v in values] + [v[1] for v in values]
        part = scatter_part(values, index_ref[:, o * capacity : (o + 1) * capacity], node_rows)
        if o == 0:
            acc_ref[...] = part
        else:
            acc_ref[...] += part
    force_ref[...] = jnp.zeros_like(force_ref)
    for h in range(node_rows):
        lanes = slice(h * LANES, (h + 1) * LANES)
        piece = acc_ref[pl.ds(h, 6, stride=node_rows), :] * 4.0
        force_ref[0:6, lanes] = piece
    wide_ref[...] = jnp.zeros_like(wide_ref)
    for z in range(n_centre):
        lanes = slice(z * node_part, (z + 1) * node_part)
        factor_rows(wide_ref, (points_ref[z] - 0.5) * inverse, lanes, True)
    for start in range(0, node_dev, 512):
        left_ref[start : start + 512, :] = jnp.transpose(wide_ref[:, start : start + 512]).astype(BF16)
    wide_ref[...] = jnp.zeros_like(wide_ref)
    for o in range(n_node):
        lanes = slice(o * centre_part, (o + 1) * centre_part)
        factor_rows(wide_ref, (centres_ref[o] - 0.5) * inverse, lanes, False)
    right_ref[...] = wide_ref[...].astype(BF16)
    wide_ref[...] = jnp.zeros_like(wide_ref)
    for o in range(n_node):
        lanes = slice(o * centre_part, (o + 1) * centre_part)
        high, low = split(coeffs_ref[o] * 4.0)
        wide_ref[0:6, lanes] = high
        wide_ref[8:14, lanes] = low
    for start in range(0, centre_dev, 512):
        coef_ref[start : start + 512, :] = jnp.transpose(wide_ref[:, start : start + 512]).astype(BF16)
    facc_ref[...] = jnp.zeros_like(facc_ref)
    tile_g, tile_j = min(256, node_dev), min(512, centre_dev)

    @pl.loop(0, node_dev // tile_g)
    def _(i):
        at = pl.ds(pl.multiple_of(i * tile_g, tile_g), tile_g)
        left = left_ref[at, :]
        force = force_ref[:, at].astype(BF16)
        disp = jnp.zeros((tile_g, LANES), F32)
        for start in range(0, centre_dev, tile_j):
            columns = slice(start, start + tile_j)
            squared = jnp.dot(left, right_ref[:, columns], preferred_element_type=F32)
            squared = jnp.maximum(squared, 1e-20)
            scaled = squared * lax.rsqrt(squared)
            remain = jnp.maximum(1.0 - scaled, 0.0)
            remain = remain * remain
            remain = remain * remain
            basis = remain * (scaled + 0.25)
            high = basis.astype(BF16)
            low = (basis - high.astype(F32)).astype(BF16)
            weights = coef_ref[columns, :]
            disp = disp + jnp.dot(high, weights, preferred_element_type=F32)
            disp = disp + jnp.dot(low, weights, preferred_element_type=F32)
            facc_ref[:, columns] += jnp.dot(force, high, preferred_element_type=F32) + jnp.dot(
                force, low, preferred_element_type=F32
            )
        dacc_ref[at, :] = disp

    part_rows = node_part // LANES
    for z in range(n_centre):
        for r in range(part_rows):
            start = z * node_part + r * LANES
            turned = jnp.transpose(dacc_ref[start : start + LANES, :])
            disp_ref[z, pl.ds(r, 6, stride=part_rows), :] = turned[0:6] + turned[8:14]
    for o in range(n_node):
        lanes = slice(o * centre_part, (o + 1) * centre_part)
        total_ref[o] = facc_ref[0:3, lanes] + facc_ref[3:6, lanes]


def reduce_kernel(
    n_node, n_centre, disp_ref, total_ref, whole_ref, force_ref,
    got_disp, got_force, mine_ref, sem_a, sem_b, sem_c,
):
    greet((("node", n_node), ("centre", n_centre)))
    me_node, me_centre = lax.axis_index("node"), lax.axis_index("centre")
    copies = spread("centre", n_centre, disp_ref, got_disp, sem_a.at[0], sem_a.at[1], False)
    later = spread("node", n_node, total_ref, got_force, sem_b.at[0], sem_b.at[1], False)
    got_disp[me_centre] = disp_ref[me_centre]
    got_force[me_node] = total_ref[me_node]
    for copy in copies:
        copy.wait()
    total = got_disp[0]
    for z in range(1, n_centre):
        total = total + got_disp[z]
    mine_ref[...] = total
    whole_ref[me_centre] = total
    copies = spread("centre", n_centre, mine_ref, whole_ref, sem_c.at[0], sem_c.at[1], True)
    for copy in later:
        copy.wait()
    total = got_force[0]
    for o in range(1, n_node):
        total = total + got_force[o]
    force_ref[...] = total
    for copy in copies:
        copy.wait()


def pick_kernel(n_node, n_centre, rows, whole_ref, index_ref, send_ref, tab_ref):
    part_rows = whole_ref.shape[1] // 6
    node_rows = part_rows * n_centre
    capacity = rows * LANES
    lhs = []
    for c in range(6):
        for z in range(n_centre):
            high, low = split(whole_ref[z, c * part_rows : (c + 1) * part_rows, :])
            tab_ref[z * part_rows : (z + 1) * part_rows, :] = high
            tab_ref[node_rows + z * part_rows : node_rows + (z + 1) * part_rows, :] = low
        lhs.append(jnp.transpose(tab_ref[...]).astype(BF16)[:, : 2 * node_rows])
    lhs = jnp.concatenate(lhs, axis=0)
    for o in range(n_node):
        got = gather_part(lhs, index_ref[:, o * capacity : (o + 1) * capacity], node_rows, 6)
        for r in range(rows):
            send_ref[o, pl.ds(r, 6, stride=rows), :] = got[:, r * LANES : (r + 1) * LANES]


def exchange_kernel(n_node, send_ref, recv_ref, sems):
    greet((("node", n_node),))
    copies = spread("node", n_node, send_ref, recv_ref, sems.at[0], sems.at[1], False)
    me = lax.axis_index("node")
    recv_ref[me] = send_ref[me]
    for copy in copies:
        copy.wait()


def place_kernel(n_node, rows, recv_ref, perm_ref, out_ref, tab_ref):
    high_rows = n_node * rows
    lhs = []
    for c in range(6):
        for o in range(n_node):
            high, low = split(recv_ref[o, c * rows : (c + 1) * rows, :])
            tab_ref[o * rows : (o + 1) * rows, :] = high
            tab_ref[high_rows + o * rows : high_rows + (o + 1) * rows, :] = low
        lhs.append(jnp.transpose(tab_ref[...]).astype(BF16))
    lhs = jnp.concatenate(lhs, axis=0)
    fluid_dev = perm_ref.shape[1]
    step = 1024
    for start in range(0, fluid_dev, step):
        out_ref[:, start : start + step] = gather_part(
            lhs, perm_ref[:, start : start + step], high_rows, 6
        )


def body(node_coords, centre_coords, disp_coef, send_count, send_order, slot_perm, fluid_force):
    n_node = lax.axis_size("node")
    n_centre = lax.axis_size("centre")
    node_dev = send_order.shape[1]
    fluid_dev = slot_perm.shape[1]
    capacity = fluid_dev // n_node
    rows = capacity // LANES
    node_rows = node_dev // LANES
    centre_part = centre_coords.shape[1]
    centre_total = centre_part * n_node * n_centre
    centre_dev = centre_part * n_node
    node_part = node_coords.shape[1]
    part_rows = node_part // LANES
    radius = (0.75 * SUPPORT / (math.pi * centre_total)) ** (1.0 / 3.0)
    dma = pltpu.SemaphoreType.DMA
    shape = jax.ShapeDtypeStruct

    def local(function, outs, n_in, scratch, name, specs=None):
        return pl.pallas_call(
            function,
            out_shape=outs,
            in_specs=specs or [vmem()] * n_in,
            out_specs=jax.tree.map(lambda _: vmem(), outs),
            scratch_shapes=scratch,
            name=name,
            compiler_params=pltpu.CompilerParams(vmem_limit_bytes=VMEM_BYTES),
        )

    def remote(function, outs, n_in, scratch, name, number):
        return pl.pallas_call(
            function,
            out_shape=outs,
            in_specs=[vmem()] * n_in,
            out_specs=jax.tree.map(lambda _: vmem(), outs),
            scratch_shapes=scratch,
            name=name,
            compiler_params=pltpu.CompilerParams(
                vmem_limit_bytes=VMEM_BYTES, collective_id=number, has_side_effects=True
            ),
        )

    sent, index = local(
        functools.partial(prepare_kernel, n_node, rows),
        (shape((n_node, 3 * rows, LANES), F32), shape((1, fluid_dev), jnp.int32)),
        4,
        [pltpu.VMEM((6 * fluid_dev // LANES, LANES), F32)],
        "prepare",
        [smem(), vmem(), vmem(), vmem()],
    )(send_count, send_order.reshape(node_rows, LANES), slot_perm, fluid_force)
    points, centres, coeffs, got = remote(
        functools.partial(gather_kernel, n_node, n_centre),
        (
            shape((n_centre, 3, node_part), F32),
            shape((n_node, 3, centre_part), F32),
            shape((n_node, 6, centre_part), F32),
            shape((n_node, 3 * rows, LANES), F32),
        ),
        4,
        [dma((2, n_centre)), dma((2, n_node)), dma((2, n_node)), dma((2, n_node))],
        "gather",
        0,
    )(node_coords, centre_coords, disp_coef, sent)
    partial, totals = local(
        functools.partial(pair_kernel, n_node, n_centre, rows, radius),
        (shape((n_centre, 6 * part_rows, LANES), F32), shape((n_node, 3, centre_part), F32)),
        5,
        [
            pltpu.VMEM((LANES, max(node_dev, centre_dev)), F32),
            pltpu.VMEM((node_dev, LANES), BF16),
            pltpu.VMEM((LANES, centre_dev), BF16),
            pltpu.VMEM((centre_dev, LANES), BF16),
            pltpu.VMEM((16, node_dev), F32),
            pltpu.VMEM((6 * node_rows, LANES), F32),
            pltpu.VMEM((16, centre_dev), F32),
            pltpu.VMEM((node_dev, LANES), F32),
        ],
        "pairs",
    )(points, centres, coeffs, got, index)
    whole, centre_force = remote(
        functools.partial(reduce_kernel, n_node, n_centre),
        (shape((n_centre, 6 * part_rows, LANES), F32), shape((3, centre_part), F32)),
        2,
        [
            pltpu.VMEM((n_centre, 6 * part_rows, LANES), F32),
            pltpu.VMEM((n_node, 3, centre_part), F32),
            pltpu.VMEM((6 * part_rows, LANES), F32),
            dma((2, n_centre)),
            dma((2, n_node)),
            dma((2, n_centre)),
        ],
        "reduce",
        1,
    )(partial, totals)
    outgoing = local(
        functools.partial(pick_kernel, n_node, n_centre, rows),
        shape((n_node, 6 * rows, LANES), F32),
        2,
        [pltpu.VMEM((LANES, LANES), F32)],
        "pick",
    )(whole, index)
    received = remote(
        functools.partial(exchange_kernel, n_node),
        shape((n_node, 6 * rows, LANES), F32),
        1,
        [dma((2, n_node))],
        "exchange",
        2,
    )(outgoing)
    fluid_disp = local(
        functools.partial(place_kernel, n_node, rows),
        shape((6, fluid_dev), F32),
        2,
        [pltpu.VMEM((LANES, LANES), F32)],
        "place",
    )(received, slot_perm)
    return (fluid_disp, centre_force)


def solution(mesh):
    placed = (
        P(None, ("node", "centre")),
        P(None, ("centre", "node")),
        P(None, ("centre", "node")),
        P("node", None),
        P("node", None),
        P("node", None),
        P(None, "node"),
    )
    return jax.shard_map(
        body,
        mesh=mesh,
        in_specs=placed,
        out_specs=(P(None, "node"), P(None, ("centre", "node"))),
        check_vma=False,
    )
```

time: 466 us -> 109 us (0.23)
  matrix products: 188 us -> 0 us
  local copies, waits for them, and re-layouts: 160 us -> 3.64 us
  Pallas kernels: 0 us -> 104 us
  other arithmetic: 55.1 us -> 0 us
  blocking collectives: 32.2 us -> 0 us
  between operations: 15.7 us -> 0.72 us
  starting transfers between devices: 8.66 us -> 0 us
  waiting for transfers between devices: 5.54 us -> 0 us
    dot_general x16 -> x0, matrix products: 188 us -> none  [the longest x8 106 us: displace(): lax.dot_general(coeffs, basis, (((1,), (1,)), ((), ())), precision=lax.Pr...]
    gather x5 -> x0, local copies, waits for them, and re-layouts: 137 us -> none  [the longest x1 45.5 us: body(): picked = send_order[0][places]]
    pallas_call x0 -> x7, Pallas kernels: none -> 104 us  [the longest x1 65.4 us: body(): local(functools.partial(pair_kernel, n_node, n_centre, rows, radius), (sh...]
    scatter-add x1 -> x0, other arithmetic: 47.1 us -> none  [body(): wall_force = jnp.zeros((3, node_dev), jnp.float32).at[:, picked].add(masked)]
    all_gather x3 -> x0, blocking collectives: 32.2 us -> none  [the longest x1 13.3 us: body(): points = lax.all_gather(node_coords, 'centre', axis=1, tiled=True)]
    all_to_all x2 -> x0, starting transfers between devices: 8.58 us -> none  [the longest x1 5.17 us: body(): lax.all_to_all(fluid_force[:, inverse], 'node', split_axis=1, concat_axis...]
    unnamed x18 -> x17, local copies, waits for them, and re-layouts: 10.7 us -> 3.64 us
    sort x1 -> x0, other arithmetic: 6.77 us -> none  [body(): inverse = jnp.argsort(ordering)]
  transfers between devices with their start and end apart: 4 -> 0, of which waited for: 2 -> 0; matrix products, arithmetic and copies ran while one was open for 69% -> 0% of each run, Pallas kernels for 0% -> 0%
where the time goes in v1:
time: 109 us; the launch traced here: 108 us
  Pallas kernels  104 us (95%)
  local copies, waits for them, and re-layouts  3.64 us (3%)
    pallas_call x1, Pallas kernels, body(): local(functools.partial(pair_kernel, n_node, n_centre, rows, radius), (sh...  65.4 us
    pallas_call x1, Pallas kernels, body(): remote(functools.partial(gather_kernel, n_node, n_centre), (shape((n_cent...  11.3 us
    pallas_call x1, Pallas kernels, body(): remote(functools.partial(reduce_kernel, n_node, n_centre), (shape((n_cent...  9.7 us
    pallas_call x1, Pallas kernels, body(): remote(functools.partial(exchange_kernel, n_node), shape((n_node, 6 * row...  6 us
    pallas_call x1, Pallas kernels, body(): local(functools.partial(place_kernel, n_node, rows), shape((6, fluid_dev)...  4.69 us
    pallas_call x1, Pallas kernels, body(): local(functools.partial(pick_kernel, n_node, n_centre, rows), shape((n_no...  3.91 us
    unnamed x17, local copies, waits for them, and re-layouts  3.64 us
    pallas_call x1, Pallas kernels, body(): local(functools.partial(prepare_kernel, n_node, rows), (shape((n_node, 3...  2.93 us

profile of v1, /device:TPU:0, one launch (start us, length us, event | category | flops | bytes accessed | tf_op | source)
XLA Modules:
  0.0 108.3 jit_solution(9348159600349383717)
XLA Ops:
  0.6 0.0 copy-start.7
  0.6 0.6 copy-done.7
  1.3 0.0 copy-start
  1.3 0.9 copy-done
  2.2 0.0 copy-start.1
  2.2 0.8 copy-done.1
  3.0 0.0 copy-start.5
  3.0 0.7 copy-done.5
  3.7 0.0 copy-start.3
  3.7 0.0 copy-start.4
  3.7 0.0 copy-start.6
  3.7 2.9 %prepare.1 = (f32[8,24,128]{2,1,0:T(8,128)S(1)}, s32[1,8192]{1,0:T(1,128)S(1)}) custom-call(s32[1,8]{1,0:T(1,128)S(1)} %copy-done.7, s32[32,128]{1,0:T(8,128)S(1)} %bitcast.1, s32[1,8192]{1,0:T(1,128)S(1)} %copy-done.1, f32[3,8192]{1,0:T(4,128)S(1)} %copy-done), custom_call_target="tpu_custom_call" | custom-call | tf_op jit(solution)/shard_map/prepare/pallas_call | solution.py:374
  6.6 0.0 copy-done.3
  6.6 0.0 copy-done.4
  6.6 0.0 copy-done.6
  6.6 11.3 %gather.1 = (f32[4,3,1024]{2,1,0:T(4,128)S(1)}, f32[8,3,512]{2,1,0:T(4,128)S(1)}, f32[8,6,512]{2,1,0:T(8,128)S(1)}, f32[8,24,128]{2,1,0:T(8,128)S(1)}) custom-call(f32[3,1024]{1,0:T(4,128)S(1)} %copy-done.3, f32[3,512]{1,0:T(4,128)S(1)} %copy-done.6, f32[6,512]{1,0:T(8,128)S(1)} %copy-done.4, f32[8,24,128]{2,1,0:T(8,128)S(1)} %get-tuple-element.12.send_ref), custom_call_target="tpu_custom_call" | custom-call | tf_op jit(solution)/shard_map/gather/pallas_call | solution.py:382
  17.9 65.4 %pairs.1 = (f32[4,48,128]{2,1,0:T(8,128)S(1)}, f32[8,3,512]{2,1,0:T(4,128)S(1)}) custom-call(f32[4,3,1024]{2,1,0:T(4,128)S(1)} %get-tuple-element.13.points_ref, f32[8,3,512]{2,1,0:T(4,128)S(1)} %get-tuple-element.14.centres_ref, f32[8,6,512]{2,1,0:T(8,128)S(1)} %get-tuple-element.15.coeffs_ref, f32[8,24,128]{2,1,0:T(8,128)S(1)} %get-tuple-element.16.recv_ref, ...), custom_call_target="tpu_custom_call" | custom-call | tf_op jit(solution)/shard_map/pairs/pallas_call | solution.py:395
  83.4 9.7 %reduce.1 = (f32[4,48,128]{2,1,0:T(8,128)S(1)}, f32[3,512]{1,0:T(4,128)S(1)}) custom-call(f32[4,48,128]{2,1,0:T(8,128)S(1)} %get-tuple-element.18.disp_ref, f32[8,3,512]{2,1,0:T(4,128)S(1)} %get-tuple-element.19.total_ref), custom_call_target="tpu_custom_call" | custom-call | tf_op jit(solution)/shard_map/reduce/pallas_call | solution.py:411
  93.1 3.9 %pick.1.send_ref = f32[8,48,128]{2,1,0:T(8,128)S(1)} custom-call(f32[4,48,128]{2,1,0:T(8,128)S(1)} %get-tuple-element.20.whole_ref, s32[1,8192]{1,0:T(1,128)S(1)} %get-tuple-element.17.index_ref), custom_call_target="tpu_custom_call" | custom-call | tf_op jit(solution)/shard_map/pick/pallas_call | solution.py:426
  97.0 0.0 copy-start.2
  97.0 6.0 %exchange.1.recv_ref = f32[8,48,128]{2,1,0:T(8,128)S(1)} custom-call(f32[8,48,128]{2,1,0:T(8,128)S(1)} %pick.1.send_ref), custom_call_target="tpu_custom_call" | custom-call | tf_op jit(solution)/shard_map/exchange/pallas_call | solution.py:433
  103.0 0.0 copy-done.2
  103.0 4.7 %place.1 = f32[6,8192]{1,0:T(8,128)} custom-call(f32[8,48,128]{2,1,0:T(8,128)S(1)} %exchange.1.recv_ref, s32[1,8192]{1,0:T(1,128)S(1)} %copy-done.2), custom_call_target="tpu_custom_call" | custom-call | tf_op jit(solution)/shard_map/place/pallas_call | solution.py:441
  107.7 0.6 copy.10
Async XLA Ops:
  0.6 0.7 copy-start.7
  1.3 0.9 copy-start
  2.2 0.8 copy-start.1
  3.0 0.7 copy-start.5
  3.7 2.9 %copy-start.3 = (f32[3,1024]{1,0:T(4,128)S(1)}, f32[3,1024]{1,0:T(4,128)}, u32[]{:S(2)}) copy-start(f32[3,1024]{1,0:T(4,128)} %node_ref.1) | copy-start | bytes 36868
  3.7 3.0 %copy-start.4 = (f32[6,512]{1,0:T(8,128)S(1)}, f32[6,512]{1,0:T(8,128)}, u32[]{:S(2)}) copy-start(f32[6,512]{1,0:T(8,128)} %coef_ref.1) | copy-start | bytes 36868
  3.7 3.0 %copy-start.6 = (f32[3,512]{1,0:T(4,128)S(1)}, f32[3,512]{1,0:T(4,128)}, u32[]{:S(2)}) copy-start(f32[3,512]{1,0:T(4,128)} %centre_ref.1) | copy-start | bytes 18436
  97.0 6.0 %copy-start.2 = (s32[1,8192]{1,0:T(1,128)S(1)}, s32[1,8192]{1,0:T(1,128)}, u32[]{:S(2)}) copy-start(s32[1,8192]{1,0:T(1,128)} %perm_ref.3) | copy-start | bytes 98308

commit v2 on v1

--- a/solution.py
+++ b/solution.py
@@ -169,19 +169,105 @@
     ref[base : base + 3, lanes] = jnp.ones((3, square.shape[1]), F32)
 
 
+BINS = 32
+
+
+def table_factor(table):
+    rows = table.shape[0]
+    high, low = split(table)
+    stacked = jnp.concatenate([high, low, jnp.zeros((LANES - 2 * rows, LANES), F32)], axis=0)
+    return jnp.transpose(stacked).astype(BF16)[:, : 2 * rows]
+
+
+def order_by(first, rank_ref):
+    count = first.shape[1]
+    bins = jnp.minimum((first * BINS).astype(jnp.int32), BINS - 1)
+    member = onehot(bins, BINS)
+    below = jnp.where(lax.broadcasted_iota(jnp.int32, (BINS, count), 0) > bins, 1.0, 0.0)
+    carry = jnp.sum(below, axis=1, keepdims=True)
+    chunks = count // LANES
+    stacked = jnp.concatenate(
+        [member[:, k * LANES : (k + 1) * LANES] for k in range(chunks)], axis=0
+    )
+    upper = jnp.where(
+        lax.broadcasted_iota(jnp.int32, (LANES, LANES), 0)
+        <= lax.broadcasted_iota(jnp.int32, (LANES, LANES), 1),
+        1.0,
+        0.0,
+    ).astype(BF16)
+    running = jnp.dot(stacked.astype(BF16), upper, preferred_element_type=F32)
+    for k in range(chunks):
+        part = running[k * BINS : (k + 1) * BINS]
+        mine = stacked[k * BINS : (k + 1) * BINS]
+        rank_ref[k : k + 1, :] = jnp.sum(mine * (part + carry), axis=0, keepdims=True) - 1.0
+        carry = carry + part[:, LANES - 1 : LANES]
+
+
+def rank_row(rank_ref, first, last):
+    return jnp.concatenate([rank_ref[k : k + 1, :] for k in range(first, last)], axis=1).astype(
+        jnp.int32
+    )
+
+
 def pair_kernel(
     n_node, n_centre, rows, radius, points_ref, centres_ref, coeffs_ref, recv_ref, index_ref,
-    disp_ref, total_ref,
+    disp_ref, total_ref, place_ref,
     wide_ref, left_ref, right_ref, coef_ref, force_ref, acc_ref, facc_ref, dacc_ref,
+    node_rank, centre_rank, node_sorted, centre_sorted, limit_ref,
 ):
     node_part = points_ref.shape[2]
     node_dev = node_part * n_centre
     centre_part = centres_ref.shape[2]
     centre_dev = centre_part * n_node
-    node_rows = node_dev // LANES
+    node_rows, centre_rows = node_dev // LANES, centre_dev // LANES
     capacity = rows * LANES
     inverse = 1.0 / radius
+    tile_g, tile_j = min(512, node_dev), min(512, centre_dev)
+    n_g, n_j = node_dev // tile_g, centre_dev // tile_j
+    order_by(jnp.concatenate([points_ref[z][0:1, :] for z in range(n_centre)], axis=1), node_rank)
+    order_by(jnp.concatenate([centres_ref[o][0:1, :] for o in range(n_node)], axis=1), centre_rank)
+
+    def thirds(value):
+        high, rest = split(value)
+        middle, low = split(rest)
+        return [piece[c : c + 1] for piece in (high, middle, low) for c in range(3)]
+
+    used = 9 * node_rows
+    for z in range(n_centre):
+        per = node_part // LANES
+        place = rank_row(node_rank, z * per, (z + 1) * per)
+        part = scatter_part(thirds(points_ref[z]), place, node_rows)
+        acc_ref[0:used, :] = part if z == 0 else acc_ref[0:used, :] + part
+    for h in range(node_rows):
+        piece = [acc_ref[pl.ds(3 * i * node_rows + h, 3, stride=node_rows), :] for i in range(3)]
+        node_sorted[0:3, h * LANES : (h + 1) * LANES] = piece[0] + piece[1] + piece[2]
+    used = 21 * centre_rows
     for o in range(n_node):
+        per = centre_part // LANES
+        place = rank_row(centre_rank, o * per, (o + 1) * per)
+        high, low = split(coeffs_ref[o] * 4.0)
+        values = thirds(centres_ref[o]) + [p[c : c + 1] for p in (high, low) for c in range(6)]
+        part = scatter_part(values, place, centre_rows)
+        acc_ref[0:used, :] = part if o == 0 else acc_ref[0:used, :] + part
+    wide_ref[...] = jnp.zeros_like(wide_ref)
+    for h in range(centre_rows):
+        lanes = slice(h * LANES, (h + 1) * LANES)
+        piece = [
+            acc_ref[pl.ds(3 * i * centre_rows + h, 3, stride=centre_rows), :] for i in range(3)
+        ]
+        centre_sorted[0:3, lanes] = piece[0] + piece[1] + piece[2]
+        wide_ref[0:6, lanes] = acc_ref[pl.ds(9 * centre_rows + h, 6, stride=centre_rows), :]
+        wide_ref[8:14, lanes] = acc_ref[pl.ds(15 * centre_rows + h, 6, stride=centre_rows), :]
+    for start in range(0, centre_dev, 512):
+        coef_ref[start : start + 512, :] = jnp.transpose(wide_ref[:, start : start + 512]).astype(BF16)
+    factor = table_factor(node_rank[...])
+    used = 6 * node_rows
+    for o in range(n_node):
+        slots = slice(o * capacity, (o + 1) * capacity)
+        index = index_ref[:, slots]
+        place = gather_part(factor, index, node_rows, 1).astype(jnp.int32)
+        place = jnp.where(index < 0, -1, place)
+        place_ref[:, slots] = place
         values = []
         for c in range(3):
             row = jnp.concatenate(
@@ -189,47 +275,54 @@
             )
             values.append(split(row))
         values = [v[0] for v in values] + [v[1] for v in values]
-        part = scatter_part(values, index_ref[:, o * capacity : (o + 1) * capacity], node_rows)
-        if o == 0:
-            acc_ref[...] = part
-        else:
-            acc_ref[...] += part
+        part = scatter_part(values, place, node_rows)
+        acc_ref[0:used, :] = part if o == 0 else acc_ref[0:used, :] + part
     force_ref[...] = jnp.zeros_like(force_ref)
     for h in range(node_rows):
         lanes = slice(h * LANES, (h + 1) * LANES)
-        piece = acc_ref[pl.ds(h, 6, stride=node_rows), :] * 4.0
-        force_ref[0:6, lanes] = piece
+        force_ref[0:6, lanes] = acc_ref[pl.ds(h, 6, stride=node_rows), :] * 4.0
     wide_ref[...] = jnp.zeros_like(wide_ref)
-    for z in range(n_centre):
-        lanes = slice(z * node_part, (z + 1) * node_part)
-        factor_rows(wide_ref, (points_ref[z] - 0.5) * inverse, lanes, True)
+    for start in range(0, node_dev, 1024):
+        lanes = slice(start, start + 1024)
+        factor_rows(wide_ref, (node_sorted[0:3, lanes] - 0.5) * inverse, lanes, True)
     for start in range(0, node_dev, 512):
         left_ref[start : start + 512, :] = jnp.transpose(wide_ref[:, start : start + 512]).astype(BF16)
     wide_ref[...] = jnp.zeros_like(wide_ref)
-    for o in range(n_node):
-        lanes = slice(o * centre_part, (o + 1) * centre_part)
-        factor_rows(wide_ref, (centres_ref[o] - 0.5) * inverse, lanes, False)
+    for start in range(0, centre_dev, 512):
+        lanes = slice(start, start + 512)
+        factor_rows(wide_ref, (centre_sorted[0:3, lanes] - 0.5) * inverse, lanes, False)
     right_ref[...] = wide_ref[...].astype(BF16)
-    wide_ref[...] = jnp.zeros_like(wide_ref)
-    for o in range(n_node):
-        lanes = slice(o * centre_part, (o + 1) * centre_part)
-        high, low = split(coeffs_ref[o] * 4.0)
-        wide_ref[0:6, lanes] = high
-        wide_ref[8:14, lanes] = low
-    for start in range(0, centre_dev, 512):
-        coef_ref[start : start + 512, :] = jnp.transpose(wide_ref[:, start : start + 512]).astype(BF16)
+    reach = radius * 1.00001
+    upto, since = [], []
+    for j in range(n_j):
+        row = centre_sorted[0:1, j * tile_j : (j + 1) * tile_j]
+        upto.append(jnp.max(row))
+        since.append(jnp.min(row))
+    for j in range(1, n_j):
+        upto[j] = jnp.maximum(upto[j], upto[j - 1])
+    for j in range(n_j - 2, -1, -1):
+        since[j] = jnp.minimum(since[j], since[j + 1])
+    for i in range(n_g):
+        row = node_sorted[0:1, i * tile_g : (i + 1) * tile_g]
+        least, most = jnp.min(row) - reach, jnp.max(row) + reach
+        before, after = jnp.int32(0), jnp.int32(n_j)
+        for j in range(n_j):
+            before = before + jnp.where(upto[j] < least, 1, 0)
+            after = after - jnp.where(since[j] > most, 1, 0)
+        limit_ref[0, i] = before
+        limit_ref[1, i] = after
     facc_ref[...] = jnp.zeros_like(facc_ref)
-    tile_g, tile_j = min(256, node_dev), min(512, centre_dev)
-
-    @pl.loop(0, node_dev // tile_g)
+    dacc_ref[...] = jnp.zeros_like(dacc_ref)
+
+    @pl.loop(0, n_g)
     def _(i):
         at = pl.ds(pl.multiple_of(i * tile_g, tile_g), tile_g)
-        left = left_ref[at, :]
-        force = force_ref[:, at].astype(BF16)
-        disp = jnp.zeros((tile_g, LANES), F32)
-        for start in range(0, centre_dev, tile_j):
-            columns = slice(start, start + tile_j)
-            squared = jnp.dot(left, right_ref[:, columns], preferred_element_type=F32)
+
+        @pl.loop(limit_ref[0, i], limit_ref[1, i])
+        def _(j):
+            columns = pl.ds(pl.multiple_of(j * tile_j, tile_j), tile_j)
+            force = force_ref[:, at].astype(BF16)
+            squared = jnp.dot(left_ref[at, :], right_ref[:, columns], preferred_element_type=F32)
             squared = jnp.maximum(squared, 1e-20)
             scaled = squared * lax.rsqrt(squared)
             remain = jnp.maximum(1.0 - scaled, 0.0)
@@ -239,12 +332,12 @@
             high = basis.astype(BF16)
             low = (basis - high.astype(F32)).astype(BF16)
             weights = coef_ref[columns, :]
-            disp = disp + jnp.dot(high, weights, preferred_element_type=F32)
-            disp = disp + jnp.dot(low, weights, preferred_element_type=F32)
+            dacc_ref[at, :] += jnp.dot(high, weights, preferred_element_type=F32) + jnp.dot(
+                low, weights, preferred_element_type=F32
+            )
             facc_ref[:, columns] += jnp.dot(force, high, preferred_element_type=F32) + jnp.dot(
                 force, low, preferred_element_type=F32
             )
-        dacc_ref[at, :] = disp
 
     part_rows = node_part // LANES
     for z in range(n_centre):
@@ -252,9 +345,17 @@
             start = z * node_part + r * LANES
             turned = jnp.transpose(dacc_ref[start : start + LANES, :])
             disp_ref[z, pl.ds(r, 6, stride=part_rows), :] = turned[0:6] + turned[8:14]
+    for h in range(centre_rows):
+        lanes = slice(h * LANES, (h + 1) * LANES)
+        acc_ref[pl.ds(h, 3, stride=centre_rows), :] = facc_ref[0:3, lanes] + facc_ref[3:6, lanes]
+    factor = jnp.concatenate(
+        [table_factor(acc_ref[c * centre_rows : (c + 1) * centre_rows, :]) for c in range(3)],
+        axis=0,
+    )
     for o in range(n_node):
-        lanes = slice(o * centre_part, (o + 1) * centre_part)
-        total_ref[o] = facc_ref[0:3, lanes] + facc_ref[3:6, lanes]
+        per = centre_part // LANES
+        place = rank_row(centre_rank, o * per, (o + 1) * per)
+        total_ref[o] = gather_part(factor, place, centre_rows, 3)
 
 
 def reduce_kernel(
@@ -392,9 +493,13 @@
         "gather",
         0,
     )(node_coords, centre_coords, disp_coef, sent)
-    partial, totals = local(
+    partial, totals, places = local(
         functools.partial(pair_kernel, n_node, n_centre, rows, radius),
-        (shape((n_centre, 6 * part_rows, LANES), F32), shape((n_node, 3, centre_part), F32)),
+        (
+            shape((n_centre, 6 * part_rows, LANES), F32),
+            shape((n_node, 3, centre_part), F32),
+            shape((1, fluid_dev), jnp.int32),
+        ),
         5,
         [
             pltpu.VMEM((LANES, max(node_dev, centre_dev)), F32),
@@ -402,9 +507,14 @@
             pltpu.VMEM((LANES, centre_dev), BF16),
             pltpu.VMEM((centre_dev, LANES), BF16),
             pltpu.VMEM((16, node_dev), F32),
-            pltpu.VMEM((6 * node_rows, LANES), F32),
+            pltpu.VMEM((max(9 * node_rows, 21 * centre_dev // LANES), LANES), F32),
             pltpu.VMEM((16, centre_dev), F32),
             pltpu.VMEM((node_dev, LANES), F32),
+            pltpu.VMEM((node_rows, LANES), F32),
+            pltpu.VMEM((centre_dev // LANES, LANES), F32),
+            pltpu.VMEM((8, node_dev), F32),
+            pltpu.VMEM((8, centre_dev), F32),
+            pltpu.SMEM((2, node_dev // min(512, node_dev)), jnp.int32),
         ],
         "pairs",
     )(points, centres, coeffs, got, index)
@@ -429,7 +539,7 @@
         2,
         [pltpu.VMEM((LANES, LANES), F32)],
         "pick",
-    )(whole, index)
+    )(whole, places)
     received = remote(
         functools.partial(exchange_kernel, n_node),
         shape((n_node, 6 * rows, LANES), F32),

time: 109 us -> 83.7 us (0.77)
  Pallas kernels: 104 us -> 78.7 us
    pallas_call x1, Pallas kernels: 65.4 us -> 37.9 us  [body(): local(functools.partial(pair_kernel, n_node, n_centre, rows, radius), (sh...]
    pallas_call x1, Pallas kernels: 9.7 us -> 12.8 us  [body(): remote(functools.partial(reduce_kernel, n_node, n_centre), (shape((n_cent...]
where the time goes in v2:
time: 83.7 us; the launch traced here: 83.1 us
  Pallas kernels  78.7 us (94%)
  local copies, waits for them, and re-layouts  3.64 us (4%)
    pallas_call x1, Pallas kernels, body(): local(functools.partial(pair_kernel, n_node, n_centre, rows, radius), (sh...  37.9 us
    pallas_call x1, Pallas kernels, body(): remote(functools.partial(reduce_kernel, n_node, n_centre), (shape((n_cent...  12.8 us
    pallas_call x1, Pallas kernels, body(): remote(functools.partial(gather_kernel, n_node, n_centre), (shape((n_cent...  11.3 us
    pallas_call x1, Pallas kernels, body(): remote(functools.partial(exchange_kernel, n_node), shape((n_node, 6 * row...  5.24 us
    pallas_call x1, Pallas kernels, body(): local(functools.partial(place_kernel, n_node, rows), shape((6, fluid_dev)...  4.69 us
    pallas_call x1, Pallas kernels, body(): local(functools.partial(pick_kernel, n_node, n_centre, rows), shape((n_no...  3.91 us
    unnamed x17, local copies, waits for them, and re-layouts  3.64 us
    pallas_call x1, Pallas kernels, body(): local(functools.partial(prepare_kernel, n_node, rows), (shape((n_node, 3...  2.93 us

profile of v2, /device:TPU:0, one launch (start us, length us, event | category | flops | bytes accessed | tf_op | source)
XLA Modules:
  0.0 83.1 jit_solution(8941176575378696657)
XLA Ops:
  0.6 0.0 copy-start.7
  0.6 0.6 copy-done.7
  1.3 0.0 copy-start
  1.3 0.9 %copy-done = f32[3,8192]{1,0:T(4,128)S(1)} copy-done((f32[3,8192]{1,0:T(4,128)S(1)}, f32[3,8192]{1,0:T(4,128)}, u32[]{:S(2)}) %copy-start) | copy-done | bytes 98328
  2.2 0.0 copy-start.1
  2.2 0.8 copy-done.1
  3.0 0.0 copy-start.5
  3.0 0.7 copy-done.5
  3.7 0.0 copy-start.3
  3.7 0.0 copy-start.4
  3.7 0.0 copy-start.6
  3.7 2.9 %prepare.1 = (f32[8,24,128]{2,1,0:T(8,128)S(1)}, s32[1,8192]{1,0:T(1,128)S(1)}) custom-call(s32[1,8]{1,0:T(1,128)S(1)} %copy-done.7, s32[32,128]{1,0:T(8,128)S(1)} %bitcast.1, s32[1,8192]{1,0:T(1,128)S(1)} %copy-done.1, f32[3,8192]{1,0:T(4,128)S(1)} %copy-done), custom_call_target="tpu_custom_call" | custom-call | tf_op jit(solution)/shard_map/prepare/pallas_call | solution.py:475
  6.6 0.0 copy-done.3
  6.6 0.0 copy-done.4
  6.6 0.0 copy-done.6
  6.6 11.3 %gather.1 = (f32[4,3,1024]{2,1,0:T(4,128)S(1)}, f32[8,3,512]{2,1,0:T(4,128)S(1)}, f32[8,6,512]{2,1,0:T(8,128)S(1)}, f32[8,24,128]{2,1,0:T(8,128)S(1)}) custom-call(f32[3,1024]{1,0:T(4,128)S(1)} %copy-done.3, f32[3,512]{1,0:T(4,128)S(1)} %copy-done.6, f32[6,512]{1,0:T(8,128)S(1)} %copy-done.4, f32[8,24,128]{2,1,0:T(8,128)S(1)} %get-tuple-element.13.send_ref), custom_call_target="tpu_custom_call" | custom-call | tf_op jit(solution)/shard_map/gather/pallas_call | solution.py:483
  17.9 37.9 %pairs.1 = (f32[4,48,128]{2,1,0:T(8,128)S(1)}, f32[8,3,512]{2,1,0:T(4,128)S(1)}, s32[1,8192]{1,0:T(1,128)S(1)}) custom-call(f32[4,3,1024]{2,1,0:T(4,128)S(1)} %get-tuple-element.14.points_ref, f32[8,3,512]{2,1,0:T(4,128)S(1)} %get-tuple-element.15.centres_ref, f32[8,6,512]{2,1,0:T(8,128)S(1)} %get-tuple-element.16.coeffs_ref, ...), custom_call_target="tpu_custom_call" | custom-call | tf_op jit(solution)/shard_map/pairs/pallas_call | solution.py:496
  55.8 12.8 %reduce.1 = (f32[4,48,128]{2,1,0:T(8,128)S(1)}, f32[3,512]{1,0:T(4,128)S(1)}) custom-call(f32[4,48,128]{2,1,0:T(8,128)S(1)} %get-tuple-element.19.disp_ref, f32[8,3,512]{2,1,0:T(4,128)S(1)} %get-tuple-element.20.total_ref), custom_call_target="tpu_custom_call" | custom-call | tf_op jit(solution)/shard_map/reduce/pallas_call | solution.py:521
  68.6 3.9 %pick.1.send_ref = f32[8,48,128]{2,1,0:T(8,128)S(1)} custom-call(f32[4,48,128]{2,1,0:T(8,128)S(1)} %get-tuple-element.21.whole_ref, s32[1,8192]{1,0:T(1,128)S(1)} %get-tuple-element.22.index_ref), custom_call_target="tpu_custom_call" | custom-call | tf_op jit(solution)/shard_map/pick/pallas_call | solution.py:536
  72.5 0.0 copy-start.2
  72.5 5.2 %exchange.1.recv_ref = f32[8,48,128]{2,1,0:T(8,128)S(1)} custom-call(f32[8,48,128]{2,1,0:T(8,128)S(1)} %pick.1.send_ref), custom_call_target="tpu_custom_call" | custom-call | tf_op jit(solution)/shard_map/exchange/pallas_call | solution.py:543
  77.8 0.0 copy-done.2
  77.8 4.7 %place.1 = f32[6,8192]{1,0:T(8,128)} custom-call(f32[8,48,128]{2,1,0:T(8,128)S(1)} %exchange.1.recv_ref, s32[1,8192]{1,0:T(1,128)S(1)} %copy-done.2), custom_call_target="tpu_custom_call" | custom-call | tf_op jit(solution)/shard_map/place/pallas_call | solution.py:551
  82.5 0.6 copy.10
Async XLA Ops:
  0.6 0.7 copy-start.7
  1.3 0.9 %copy-start = (f32[3,8192]{1,0:T(4,128)S(1)}, f32[3,8192]{1,0:T(4,128)}, u32[]{:S(2)}) copy-start(f32[3,8192]{1,0:T(4,128)} %force_ref.1) | copy-start | bytes 294916
  2.2 0.8 copy-start.1
  3.0 0.7 copy-start.5
  3.7 2.9 %copy-start.3 = (f32[3,1024]{1,0:T(4,128)S(1)}, f32[3,1024]{1,0:T(4,128)}, u32[]{:S(2)}) copy-start(f32[3,1024]{1,0:T(4,128)} %node_ref.1) | copy-start | bytes 36868
  3.7 3.0 %copy-start.4 = (f32[6,512]{1,0:T(8,128)S(1)}, f32[6,512]{1,0:T(8,128)}, u32[]{:S(2)}) copy-start(f32[6,512]{1,0:T(8,128)} %coef_ref.1) | copy-start | bytes 36868
  3.7 3.0 %copy-start.6 = (f32[3,512]{1,0:T(4,128)S(1)}, f32[3,512]{1,0:T(4,128)}, u32[]{:S(2)}) copy-start(f32[3,512]{1,0:T(4,128)} %centre_ref.1) | copy-start | bytes 18436
  72.5 5.3 %copy-start.2 = (s32[1,8192]{1,0:T(1,128)S(1)}, s32[1,8192]{1,0:T(1,128)}, u32[]{:S(2)}) copy-start(s32[1,8192]{1,0:T(1,128)} %perm_ref.3) | copy-start | bytes 98308

commit v3 on v2

--- a/solution.py
+++ b/solution.py
@@ -63,11 +63,9 @@
     return jnp.concatenate(rows, axis=0)
 
 
-def prepare_kernel(n_node, rows, count_ref, order_ref, perm_ref, force_ref, send_ref, index_ref, acc_ref):
+def fill_slots(n_node, rows, perm_ref, force_ref, send_ref, acc_ref):
     fluid_dev = perm_ref.shape[1]
     high_rows = fluid_dev // LANES
-    node_rows = order_ref.shape[0]
-    capacity = rows * LANES
     step = 1024
     for start in range(0, fluid_dev, step):
         values = []
@@ -86,6 +84,11 @@
                 acc_ref[lo : lo + rows, :]
                 + acc_ref[lo + high_rows : lo + high_rows + rows, :]
             )
+
+
+def find_nodes(n_node, rows, count_ref, order_ref, index_ref):
+    node_rows = order_ref.shape[0]
+    capacity = rows * LANES
     high, low = split(order_ref[...].astype(F32))
     lhs = jnp.transpose(
         jnp.concatenate([high, low, jnp.zeros((LANES - 2 * node_rows, LANES), F32)], axis=0)
@@ -134,19 +137,31 @@
 
 
 def gather_kernel(
-    n_node, n_centre, node_ref, centre_ref, coef_ref, send_ref,
-    points_ref, centres_ref, coeffs_ref, recv_ref, sem_a, sem_b, sem_c, sem_d,
+    n_node, n_centre, rows, node_ref, centre_ref, coef_ref, count_ref, order_in, perm_in, force_in,
+    points_ref, centres_ref, coeffs_ref, recv_ref, index_ref,
+    order_ref, perm_ref, force_ref, send_ref, acc_ref, sem_a, sem_b, sem_c, sem_d, sem_in,
 ):
+    loads = [
+        pltpu.make_async_copy(perm_in, perm_ref, sem_in.at[0]),
+        pltpu.make_async_copy(force_in, force_ref, sem_in.at[1]),
+        pltpu.make_async_copy(order_in, order_ref, sem_in.at[2]),
+    ]
+    for load in loads:
+        load.start()
     greet((("node", n_node), ("centre", n_centre)))
     copies = spread("centre", n_centre, node_ref, points_ref, sem_a.at[0], sem_a.at[1], True)
     copies += spread("node", n_node, centre_ref, centres_ref, sem_b.at[0], sem_b.at[1], True)
     copies += spread("node", n_node, coef_ref, coeffs_ref, sem_c.at[0], sem_c.at[1], True)
+    for load in loads:
+        load.wait()
+    fill_slots(n_node, rows, perm_ref, force_ref, send_ref, acc_ref)
     copies += spread("node", n_node, send_ref, recv_ref, sem_d.at[0], sem_d.at[1], False)
     me_node, me_centre = lax.axis_index("node"), lax.axis_index("centre")
     points_ref[me_centre] = node_ref[...]
     centres_ref[me_node] = centre_ref[...]
     coeffs_ref[me_node] = coef_ref[...]
     recv_ref[me_node] = send_ref[me_node]
+    find_nodes(n_node, rows, count_ref, order_ref, index_ref)
     for copy in copies:
         copy.wait()
 
@@ -359,8 +374,8 @@
 
 
 def reduce_kernel(
-    n_node, n_centre, disp_ref, total_ref, whole_ref, force_ref,
-    got_disp, got_force, mine_ref, sem_a, sem_b, sem_c,
+    n_node, n_centre, rows, disp_ref, total_ref, index_ref, recv_ref, force_ref,
+    got_disp, got_force, mine_ref, whole_ref, send_ref, tab_ref, sem_a, sem_b, sem_c, sem_d,
 ):
     greet((("node", n_node), ("centre", n_centre)))
     me_node, me_centre = lax.axis_index("node"), lax.axis_index("centre")
@@ -384,31 +399,37 @@
     force_ref[...] = total
     for copy in copies:
         copy.wait()
-
-
-def pick_kernel(n_node, n_centre, rows, whole_ref, index_ref, send_ref, tab_ref):
     part_rows = whole_ref.shape[1] // 6
     node_rows = part_rows * n_centre
     capacity = rows * LANES
-    lhs = []
+    factor = []
     for c in range(6):
         for z in range(n_centre):
-            high, low = split(whole_ref[z, c * part_rows : (c + 1) * part_rows, :])
-            tab_ref[z * part_rows : (z + 1) * part_rows, :] = high
-            tab_ref[node_rows + z * part_rows : node_rows + (z + 1) * part_rows, :] = low
-        lhs.append(jnp.transpose(tab_ref[...]).astype(BF16)[:, : 2 * node_rows])
-    lhs = jnp.concatenate(lhs, axis=0)
-    for o in range(n_node):
-        got = gather_part(lhs, index_ref[:, o * capacity : (o + 1) * capacity], node_rows, 6)
+            tab_ref[z * part_rows : (z + 1) * part_rows, :] = whole_ref[
+                z, c * part_rows : (c + 1) * part_rows, :
+            ]
+        factor.append(table_factor(tab_ref[...]))
+    factor = jnp.concatenate(factor, axis=0)
+    copies = []
+    for d in list(range(1, n_node)) + [0]:
+        peer = lax.rem(me_node + d, n_node)
+        slots = pl.ds(pl.multiple_of(peer * capacity, LANES), capacity)
+        got = gather_part(factor, index_ref[:, slots], node_rows, 6)
         for r in range(rows):
-            send_ref[o, pl.ds(r, 6, stride=rows), :] = got[:, r * LANES : (r + 1) * LANES]
-
-
-def exchange_kernel(n_node, send_ref, recv_ref, sems):
-    greet((("node", n_node),))
-    copies = spread("node", n_node, send_ref, recv_ref, sems.at[0], sems.at[1], False)
-    me = lax.axis_index("node")
-    recv_ref[me] = send_ref[me]
+            send_ref[d, pl.ds(r, 6, stride=rows), :] = got[:, r * LANES : (r + 1) * LANES]
+        if d == 0:
+            continue
+        copy = pltpu.make_async_remote_copy(
+            src_ref=send_ref.at[d],
+            dst_ref=recv_ref.at[me_node],
+            send_sem=sem_d.at[0, d],
+            recv_sem=sem_d.at[1, d],
+            device_id={"node": peer},
+            device_id_type=pl.DeviceIdType.MESH,
+        )
+        copy.start()
+        copies.append(copy)
+    recv_ref[me_node] = send_ref[0]
     for copy in copies:
         copy.wait()
 
@@ -459,11 +480,11 @@
             compiler_params=pltpu.CompilerParams(vmem_limit_bytes=VMEM_BYTES),
         )
 
-    def remote(function, outs, n_in, scratch, name, number):
+    def remote(function, outs, n_in, scratch, name, number, specs=None):
         return pl.pallas_call(
             function,
             out_shape=outs,
-            in_specs=[vmem()] * n_in,
+            in_specs=specs or [vmem()] * n_in,
             out_specs=jax.tree.map(lambda _: vmem(), outs),
             scratch_shapes=scratch,
             name=name,
@@ -472,27 +493,36 @@
             ),
         )
 
-    sent, index = local(
-        functools.partial(prepare_kernel, n_node, rows),
-        (shape((n_node, 3 * rows, LANES), F32), shape((1, fluid_dev), jnp.int32)),
-        4,
-        [pltpu.VMEM((6 * fluid_dev // LANES, LANES), F32)],
-        "prepare",
-        [smem(), vmem(), vmem(), vmem()],
-    )(send_count, send_order.reshape(node_rows, LANES), slot_perm, fluid_force)
-    points, centres, coeffs, got = remote(
-        functools.partial(gather_kernel, n_node, n_centre),
+    anywhere = pl.BlockSpec(memory_space=pl.ANY)
+    points, centres, coeffs, got, index = remote(
+        functools.partial(gather_kernel, n_node, n_centre, rows),
         (
             shape((n_centre, 3, node_part), F32),
             shape((n_node, 3, centre_part), F32),
             shape((n_node, 6, centre_part), F32),
             shape((n_node, 3 * rows, LANES), F32),
+            shape((1, fluid_dev), jnp.int32),
         ),
-        4,
-        [dma((2, n_centre)), dma((2, n_node)), dma((2, n_node)), dma((2, n_node))],
+        7,
+        [
+            pltpu.VMEM((node_rows, LANES), jnp.int32),
+            pltpu.VMEM((1, fluid_dev), jnp.int32),
+            pltpu.VMEM((3, fluid_dev), F32),
+            pltpu.VMEM((n_node, 3 * rows, LANES), F32),
+            pltpu.VMEM((6 * fluid_dev // LANES, LANES), F32),
+            dma((2, n_centre)),
+            dma((2, n_node)),
+            dma((2, n_node)),
+            dma((2, n_node)),
+            dma((3,)),
+        ],
         "gather",
         0,
-    )(node_coords, centre_coords, disp_coef, sent)
+        [vmem(), vmem(), vmem(), smem(), anywhere, anywhere, anywhere],
+    )(
+        node_coords, centre_coords, disp_coef, send_count,
+        send_order.reshape(node_rows, LANES), slot_perm, fluid_force,
+    )
     partial, totals, places = local(
         functools.partial(pair_kernel, n_node, n_centre, rows, radius),
         (
@@ -518,36 +548,25 @@
         ],
         "pairs",
     )(points, centres, coeffs, got, index)
-    whole, centre_force = remote(
-        functools.partial(reduce_kernel, n_node, n_centre),
-        (shape((n_centre, 6 * part_rows, LANES), F32), shape((3, centre_part), F32)),
-        2,
+    received, centre_force = remote(
+        functools.partial(reduce_kernel, n_node, n_centre, rows),
+        (shape((n_node, 6 * rows, LANES), F32), shape((3, centre_part), F32)),
+        3,
         [
             pltpu.VMEM((n_centre, 6 * part_rows, LANES), F32),
             pltpu.VMEM((n_node, 3, centre_part), F32),
             pltpu.VMEM((6 * part_rows, LANES), F32),
+            pltpu.VMEM((n_centre, 6 * part_rows, LANES), F32),
+            pltpu.VMEM((n_node, 6 * rows, LANES), F32),
+            pltpu.VMEM((node_rows, LANES), F32),
             dma((2, n_centre)),
             dma((2, n_node)),
             dma((2, n_centre)),
+            dma((2, n_node)),
         ],
         "reduce",
         1,
-    )(partial, totals)
-    outgoing = local(
-        functools.partial(pick_kernel, n_node, n_centre, rows),
-        shape((n_node, 6 * rows, LANES), F32),
-        2,
-        [pltpu.VMEM((LANES, LANES), F32)],
-        "pick",
-    )(whole, places)
-    received = remote(
-        functools.partial(exchange_kernel, n_node),
-        shape((n_node, 6 * rows, LANES), F32),
-        1,
-        [dma((2, n_node))],
-        "exchange",
-        2,
-    )(outgoing)
+    )(partial, totals, places)
     fluid_disp = local(
         functools.partial(place_kernel, n_node, rows),
         shape((6, fluid_dev), F32),

time: 83.7 us -> 81.7 us (0.976)
  Pallas kernels: 78.7 us -> 74.9 us
  local copies, waits for them, and re-layouts: 3.64 us -> 5.76 us
    pallas_call x5 -> x2, Pallas kernels: 36.1 us -> 32.4 us  [the longest x1 19.5 us: body(): remote(functools.partial(reduce_kernel, n_node, n_centre, rows), (shape((...]
    unnamed x17, local copies, waits for them, and re-layouts: 3.64 us -> 5.76 us
where the time goes in v3:
time: 81.7 us; the launch traced here: 81.3 us
  Pallas kernels  74.9 us (92%)
  local copies, waits for them, and re-layouts  5.76 us (7%)
    pallas_call x1, Pallas kernels, body(): local(functools.partial(pair_kernel, n_node, n_centre, rows, radius), (sh...  37.8 us
    pallas_call x1, Pallas kernels, body(): remote(functools.partial(reduce_kernel, n_node, n_centre, rows), (shape((...  19.5 us
    pallas_call x1, Pallas kernels, body(): remote(functools.partial(gather_kernel, n_node, n_centre, rows), (shape((...  12.9 us
    unnamed x17, local copies, waits for them, and re-layouts  5.76 us
    pallas_call x1, Pallas kernels, body(): local(functools.partial(place_kernel, n_node, rows), shape((6, fluid_dev)...  4.69 us

profile of v3, /device:TPU:0, one launch (start us, length us, event | category | flops | bytes accessed | tf_op | source)
XLA Modules:
  0.0 81.3 jit_solution(11704032767204630458)
XLA Ops:
  0.6 0.0 copy-start.7
  0.6 0.6 copy-done.7
  1.3 0.0 copy-start
  1.3 0.9 %copy-done = f32[3,8192]{1,0:T(4,128)S(1)} copy-done((f32[3,8192]{1,0:T(4,128)S(1)}, f32[3,8192]{1,0:T(4,128)}, u32[]{:S(2)}) %copy-start) | copy-done | bytes 98328
  2.2 0.0 copy-start.1
  2.2 0.8 copy-done.1
  3.0 0.0 copy-start.3
  3.0 0.7 copy-done.3
  3.7 0.0 copy-start.4
  3.7 0.7 copy-done.4
  4.4 0.0 copy-start.5
  4.4 0.7 copy-done.5
  5.1 0.0 copy-start.6
  5.1 0.7 copy-done.6
  5.8 12.9 %gather.1 = (f32[4,3,1024]{2,1,0:T(4,128)S(1)}, f32[8,3,512]{2,1,0:T(4,128)S(1)}, f32[8,6,512]{2,1,0:T(8,128)S(1)}, f32[8,24,128]{2,1,0:T(8,128)S(1)}, s32[1,8192]{1,0:T(1,128)S(1)}) custom-call(f32[3,1024]{1,0:T(4,128)S(1)} %copy-done.3, f32[3,512]{1,0:T(4,128)S(1)} %copy-done.6, f32[6,512]{1,0:T(8,128)S(1)} %copy-done.4, s32[1,8]{1,0:T(1,128)S(1)} %copy-done.7, ...), custom_call_target="tpu_custom_call" | custom-call | tf_op jit(solution)/shard_map/gather/pallas_call | solution.py:497
  18.7 37.8 %pairs.1 = (f32[4,48,128]{2,1,0:T(8,128)S(1)}, f32[8,3,512]{2,1,0:T(4,128)S(1)}, s32[1,8192]{1,0:T(1,128)S(1)}) custom-call(f32[4,3,1024]{2,1,0:T(4,128)S(1)} %get-tuple-element.12.points_ref, f32[8,3,512]{2,1,0:T(4,128)S(1)} %get-tuple-element.13.centres_ref, f32[8,6,512]{2,1,0:T(8,128)S(1)} %get-tuple-element.14.coeffs_ref, ...), custom_call_target="tpu_custom_call" | custom-call | tf_op jit(solution)/shard_map/pairs/pallas_call | solution.py:526
  56.5 0.0 copy-start.2
  56.5 19.5 %reduce.1 = (f32[8,48,128]{2,1,0:T(8,128)S(1)}, f32[3,512]{1,0:T(4,128)S(1)}) custom-call(f32[4,48,128]{2,1,0:T(8,128)S(1)} %get-tuple-element.17.disp_ref, f32[8,3,512]{2,1,0:T(4,128)S(1)} %get-tuple-element.18.total_ref, s32[1,8192]{1,0:T(1,128)S(1)} %get-tuple-element.19.index_ref), custom_call_target="tpu_custom_call" | custom-call | tf_op jit(solution)/shard_map/reduce/pallas_call | solution.py:551
  76.0 0.0 copy-done.2
  76.0 4.7 %place.1 = f32[6,8192]{1,0:T(8,128)} custom-call(f32[8,48,128]{2,1,0:T(8,128)S(1)} %get-tuple-element.20.recv_ref, s32[1,8192]{1,0:T(1,128)S(1)} %copy-done.2), custom_call_target="tpu_custom_call" | custom-call | tf_op jit(solution)/shard_map/place/pallas_call | solution.py:570
  80.7 0.6 copy.10
Async XLA Ops:
  0.6 0.7 copy-start.7
  1.3 0.9 %copy-start = (f32[3,8192]{1,0:T(4,128)S(1)}, f32[3,8192]{1,0:T(4,128)}, u32[]{:S(2)}) copy-start(f32[3,8192]{1,0:T(4,128)} %force_in.1) | copy-start | bytes 294916
  2.2 0.8 copy-start.1
  3.0 0.7 copy-start.3
  3.7 0.7 copy-start.4
  4.4 0.7 copy-start.5
  5.1 0.7 copy-start.6
  56.5 19.5 %copy-start.2 = (s32[1,8192]{1,0:T(1,128)S(1)}, s32[1,8192]{1,0:T(1,128)}, u32[]{:S(2)}) copy-start(s32[1,8192]{1,0:T(1,128)} %perm_ref.1) | copy-start | bytes 98308

commit v4 on v3

--- a/solution.py
+++ b/solution.py
@@ -12,7 +12,8 @@
 LANES = 128
 F32 = jnp.float32
 BF16 = jnp.bfloat16
-VMEM_BYTES = 48 * 1024 * 1024
+VMEM_BYTES = 64 * 1024 * 1024 - 512 * 1024
+WHOLE_VMEM = VMEM_BYTES
 NT = (((1,), (1,)), ((), ()))
 
 
@@ -145,6 +146,9 @@
         pltpu.make_async_copy(perm_in, perm_ref, sem_in.at[0]),
         pltpu.make_async_copy(force_in, force_ref, sem_in.at[1]),
         pltpu.make_async_copy(order_in, order_ref, sem_in.at[2]),
+        pltpu.make_async_copy(node_ref, points_ref.at[lax.axis_index("centre")], sem_in.at[3]),
+        pltpu.make_async_copy(centre_ref, centres_ref.at[lax.axis_index("node")], sem_in.at[4]),
+        pltpu.make_async_copy(coef_ref, coeffs_ref.at[lax.axis_index("node")], sem_in.at[5]),
     ]
     for load in loads:
         load.start()
@@ -156,10 +160,7 @@
         load.wait()
     fill_slots(n_node, rows, perm_ref, force_ref, send_ref, acc_ref)
     copies += spread("node", n_node, send_ref, recv_ref, sem_d.at[0], sem_d.at[1], False)
-    me_node, me_centre = lax.axis_index("node"), lax.axis_index("centre")
-    points_ref[me_centre] = node_ref[...]
-    centres_ref[me_node] = centre_ref[...]
-    coeffs_ref[me_node] = coef_ref[...]
+    me_node = lax.axis_index("node")
     recv_ref[me_node] = send_ref[me_node]
     find_nodes(n_node, rows, count_ref, order_ref, index_ref)
     for copy in copies:
@@ -480,7 +481,7 @@
             compiler_params=pltpu.CompilerParams(vmem_limit_bytes=VMEM_BYTES),
         )
 
-    def remote(function, outs, n_in, scratch, name, number, specs=None):
+    def remote(function, outs, n_in, scratch, name, number, specs=None, limit=VMEM_BYTES):
         return pl.pallas_call(
             function,
             out_shape=outs,
@@ -489,11 +490,11 @@
             scratch_shapes=scratch,
             name=name,
             compiler_params=pltpu.CompilerParams(
-                vmem_limit_bytes=VMEM_BYTES, collective_id=number, has_side_effects=True
+                vmem_limit_bytes=limit, collective_id=number, has_side_effects=True
             ),
         )
 
-    anywhere = pl.BlockSpec(memory_space=pl.ANY)
+    far = pl.BlockSpec(memory_space=pltpu.HBM)
     points, centres, coeffs, got, index = remote(
         functools.partial(gather_kernel, n_node, n_centre, rows),
         (
@@ -514,11 +515,12 @@
             dma((2, n_node)),
             dma((2, n_node)),
             dma((2, n_node)),
-            dma((3,)),
+            dma((6,)),
         ],
         "gather",
         0,
-        [vmem(), vmem(), vmem(), smem(), anywhere, anywhere, anywhere],
+        [far, far, far, smem(), far, far, far],
+        WHOLE_VMEM,
     )(
         node_coords, centre_coords, disp_coef, send_count,
         send_order.reshape(node_rows, LANES), slot_perm, fluid_force,

time: 81.7 us -> 81 us (level)
  local copies, waits for them, and re-layouts: 5.76 us -> 0.6 us
  Pallas kernels: 74.9 us -> 79.5 us
    unnamed x17 -> x3, local copies, waits for them, and re-layouts: 5.76 us -> 0.6 us
    pallas_call x1, Pallas kernels: 19.5 us -> 21.7 us  [body(): remote(functools.partial(reduce_kernel, n_node, n_centre, rows), (shape((...]
    pallas_call x1, Pallas kernels: 4.69 us -> 5.63 us  [body(): local(functools.partial(place_kernel, n_node, rows), shape((6, fluid_dev)...]
where the time goes in v4:
time: 81 us; the launch traced here: 80.8 us
  Pallas kernels  79.5 us (98%)
    pallas_call x1, Pallas kernels, body(): local(functools.partial(pair_kernel, n_node, n_centre, rows, radius), (sh...  38.6 us
    pallas_call x1, Pallas kernels, body(): remote(functools.partial(reduce_kernel, n_node, n_centre, rows), (shape((...  21.7 us
    pallas_call x1, Pallas kernels, body(): remote(functools.partial(gather_kernel, n_node, n_centre, rows), (shape((...  13.6 us
    pallas_call x1, Pallas kernels, body(): local(functools.partial(place_kernel, n_node, rows), shape((6, fluid_dev)...  5.63 us

profile of v4, /device:TPU:0, one launch (start us, length us, event | category | flops | bytes accessed | tf_op | source)
XLA Modules:
  0.0 80.8 jit_solution(17189503203602018132)
XLA Ops:
  0.6 13.6 %gather.1 = (f32[4,3,1024]{2,1,0:T(4,128)}, f32[8,3,512]{2,1,0:T(4,128)}, f32[8,6,512]{2,1,0:T(8,128)}, f32[8,24,128]{2,1,0:T(8,128)}, s32[1,8192]{1,0:T(1,128)}) custom-call(f32[3,1024]{1,0:T(4,128)} %node_ref.1, f32[3,512]{1,0:T(4,128)} %centre_ref.1, f32[6,512]{1,0:T(8,128)} %coef_ref.1, s32[1,8]{1,0:T(1,128)} %count_ref.1, s32[32,128]{1,0:T(8,128)} %bitcast.1, ...), custom_call_target="tpu_custom_call" | custom-call | tf_op jit(solution)/shard_map/gather/pallas_call | solution.py:498
  14.2 38.6 %pairs.1 = (f32[4,48,128]{2,1,0:T(8,128)}, f32[8,3,512]{2,1,0:T(4,128)}, s32[1,8192]{1,0:T(1,128)}) custom-call(f32[4,3,1024]{2,1,0:T(4,128)} %get-tuple-element.12.points_ref, f32[8,3,512]{2,1,0:T(4,128)} %get-tuple-element.13.centres_ref, f32[8,6,512]{2,1,0:T(8,128)} %get-tuple-element.14.coeffs_ref, f32[8,24,128]{2,1,0:T(8,128)} %get-tuple-element.15.recv_ref, ...), custom_call_target="tpu_custom_call" | custom-call | tf_op jit(solution)/shard_map/pairs/pallas_call | solution.py:528
  52.8 21.7 %reduce.1 = (f32[8,48,128]{2,1,0:T(8,128)}, f32[3,512]{1,0:T(4,128)}) custom-call(f32[4,48,128]{2,1,0:T(8,128)} %get-tuple-element.17.disp_ref, f32[8,3,512]{2,1,0:T(4,128)} %get-tuple-element.18.total_ref, s32[1,8192]{1,0:T(1,128)} %get-tuple-element.19.index_ref), custom_call_target="tpu_custom_call" | custom-call | tf_op jit(solution)/shard_map/reduce/pallas_call | solution.py:553
  74.5 0.0 copy-start
  74.6 5.6 %place.1 = f32[6,8192]{1,0:T(8,128)} custom-call(f32[8,48,128]{2,1,0:T(8,128)} %get-tuple-element.20.recv_ref, s32[1,8192]{1,0:T(1,128)} %perm_ref.1), custom_call_target="tpu_custom_call" | custom-call | tf_op jit(solution)/shard_map/place/pallas_call | solution.py:572
  80.2 0.0 copy-done
  80.2 0.6 copy.10
Async XLA Ops:
  74.5 5.6 %copy-start = (f32[3,512]{1,0:T(4,128)S(1)}, f32[3,512]{1,0:T(4,128)}, u32[]{:S(2)}) copy-start(f32[3,512]{1,0:T(4,128)} %get-tuple-element.25) | copy-start | bytes 18436
